TPU v7x, 32 devices: a whole 2x2x4 slice. The times are simulated.
32 devices in a mesh: dp: 8 (over y, x, core), tensor: 4 (over z).
Axes of the slice: x: 2, y: 2, z: 4, core: 2. Of those that a mesh axis runs over, the one named last changes fastest.
Arguments:
- tokens: bfloat16 [8192, 2048], P(('dp', 'tensor')), may hold values from -6 to 6
- attn_gain: bfloat16 [2048], replicated, may hold values from 0.099609375 to 1.8984375
- query_gain: bfloat16 [2048], P('tensor'), may hold values from 0.099609375 to 1.8984375
- key_gain: bfloat16 [2048], P('tensor'), may hold values from 0.099609375 to 1.8984375
- query_weight: bfloat16 [2048, 2048], P('dp', 'tensor'), may hold values from -0.125 to 0.125
- key_weight: bfloat16 [2048, 2048], P('dp', 'tensor'), may hold values from -0.125 to 0.125
- value_weight: bfloat16 [2048, 2048], P('dp', 'tensor'), may hold values from -0.125 to 0.125
- output_weight: bfloat16 [2048, 2048], P('tensor', 'dp'), may hold values from -2 to 2
- mlp_gain: bfloat16 [2048], replicated, may hold values from 0.099609375 to 1.8984375
- router_weight: bfloat16 [2048, 16], P('dp'), may hold values from -0.046875 to 0.046875
- gate_weight: bfloat16 [16, 2048, 1024], P(None, 'dp', 'tensor'), may hold values from -0.125 to 0.125
- up_weight: bfloat16 [16, 2048, 1024], P(None, 'dp', 'tensor'), may hold values from -0.125 to 0.125
- down_weight: bfloat16 [16, 1024, 2048], P(None, 'tensor', 'dp'), may hold values from -1.5 to 1.5
- query_lower: bfloat16 [8, 2048, 16], replicated, may hold values from -0.125 to 0.125
- query_raise: bfloat16 [8, 16, 2048], P(None, None, 'tensor'), may hold values from -0.75 to 0.75
- key_lower: bfloat16 [8, 2048, 16], replicated, may hold values from -0.125 to 0.125
- key_raise: bfloat16 [8, 16, 2048], P(None, None, 'tensor'), may hold values from -0.75 to 0.75
- value_lower: bfloat16 [8, 2048, 16], replicated, may hold values from -0.125 to 0.125
- value_raise: bfloat16 [8, 16, 2048], P(None, None, 'tensor'), may hold values from -0.75 to 0.75
- output_lower: bfloat16 [8, 2048, 16], P(None, 'tensor'), may hold values from -2 to 2
- output_raise: bfloat16 [8, 16, 2048], replicated, may hold values from -0.75 to 0.75
- routes: int32 [8192, 8], P('dp'), may hold values from 0 to 15, all different within a row; in each aligned block of 1024 rows (0 to 1023, 1024 to 2047, ...) at most 768 rows name the same one
- adapter_choice_rows: int32 [8], P('dp'), may hold values from 0 to 7
- out_cotangent: bfloat16 [8192, 2048], P(('dp', 'tensor')), may hold values from -6 to 6
Outputs:
- block_out: bfloat16 [8192, 2048], P(('dp', 'tensor'))
- input_grad: bfloat16 [8192, 2048], P(('dp', 'tensor'))
- grad_query_lower: float32 [8, 2048, 16], replicated
- grad_query_raise: float32 [8, 16, 2048], P(None, None, 'tensor')
- grad_key_lower: float32 [8, 2048, 16], replicated
- grad_key_raise: float32 [8, 16, 2048], P(None, None, 'tensor')
- grad_value_lower: float32 [8, 2048, 16], replicated
- grad_value_raise: float32 [8, 16, 2048], P(None, None, 'tensor')
- grad_output_lower: float32 [8, 2048, 16], P(None, 'tensor')
- grad_output_raise: float32 [8, 16, 2048], replicated
Inputs may be any that keep to these rules, and one draw needn't show every extreme that they name: `routes`: each row names 8 different experts. In each aligned block of 1024 rows (the tokens of one index of dp) no expert is named by more than 768 rows, and in some block one expert is named by exactly 768 rows.
All inputs are finite; a program needn't handle non-finite values.
Results may differ from a plain program's by a relative error of at most 0.02.
Values may be sent and summed in bfloat16 or wider, within the bound.
No kernel may reach another device: no remote copies, remote signals or barrier semaphores. Data moves between devices by JAX's collectives and lax.ppermute only.
A program may use at most 256 MiB of HBM per device.

v0:
```python
import jax
import jax.numpy as jnp
from jax import lax
from jax.sharding import PartitionSpec as P

D = 2048
HEAD_DIM = 128
EXPERTS = 16
ADAPTERS = 8
SEQUENCE_TOKENS = 1024
SEQUENCES_PER_DATA = 1
GROUP_TOK = 1024


EPSILON = 1e-05
ROPE_BASE = 10000.0
PRECISION_BEST = lax.Precision.HIGHEST
MASKED = -1e30


def norm_rows(values, gain_row):
    inverse = lax.rsqrt(jnp.mean(values * values, axis=-1, keepdims=True) + EPSILON)
    return values * inverse * gain_row


def rope_tables(row_count):
    position = (jnp.arange(row_count, dtype=jnp.int32) % SEQUENCE_TOKENS).astype(jnp.float32)
    frequency = ROPE_BASE ** (-2.0 * jnp.arange(HEAD_DIM // 2, dtype=jnp.float32) / HEAD_DIM)
    angles = position[:, None] * frequency[None, :]
    return (jnp.cos(angles), jnp.sin(angles))


def rotate(head_rows, cosine_table, sine_table):
    half_dim = HEAD_DIM // 2
    former = head_rows[..., :half_dim]
    latter = head_rows[..., half_dim:]
    cos_wide = cosine_table[:, None, :]
    sin_wide = sine_table[:, None, :]
    return jnp.concatenate(
        [former * cos_wide - latter * sin_wide, latter * cos_wide + former * sin_wide], axis=-1
    )


def matmul(left, right):
    return jnp.dot(left, right, preferred_element_type=jnp.float32)


def matmul_back(left, right):
    return lax.dot_general(
        left, right, (((1,), (1,)), ((), ())), preferred_element_type=jnp.float32
    )


def precise_setting(form, left, right):
    return jnp.einsum(
        form, left, right, precision=PRECISION_BEST, preferred_element_type=jnp.float32
    )


def select(onehot, table_rows):
    return jnp.einsum("sn,nab->sab", onehot, table_rows, preferred_element_type=jnp.float32)


def fetch_attention(query_weight, key_weight, value_weight, output_weight, router_weight):
    return (
        lax.all_gather(query_weight, "dp", axis=0, tiled=True),
        lax.all_gather(key_weight, "dp", axis=0, tiled=True),
        lax.all_gather(value_weight, "dp", axis=0, tiled=True),
        lax.all_gather(output_weight, "dp", axis=1, tiled=True),
        lax.all_gather(router_weight, "dp", axis=0, tiled=True),
    )


def per_device(
    tokens,
    attn_gain,
    query_gain,
    key_gain,
    query_weight,
    key_weight,
    value_weight,
    output_weight,
    mlp_gain,
    router_weight,
    gate_weight,
    up_weight,
    down_weight,
    query_lower,
    query_raise,
    key_lower,
    key_raise,
    value_lower,
    value_raise,
    output_lower,
    output_raise,
    routes,
    adapter_choice_rows,
    out_cotangent,
):
    local_rows = tokens.shape[0]
    width_local_shard = query_weight.shape[1]
    local_heads = width_local_shard // HEAD_DIM
    first_row = lax.axis_index("tensor") * local_rows
    block_rows = min(512, SEQUENCE_TOKENS)
    blocks = SEQUENCE_TOKENS // block_rows
    scale_factor = HEAD_DIM ** (-0.5)
    positions = jnp.arange(SEQUENCES_PER_DATA * blocks, dtype=jnp.int32)
    cosine_table, sine_table = rope_tables(GROUP_TOK)
    onehot = (
        adapter_choice_rows[:, None] == jnp.arange(ADAPTERS, dtype=jnp.int32)[None, :]
    ).astype(jnp.bfloat16)
    onehot_wide = onehot.astype(jnp.float32)

    def spread(sequence_adapter):
        return precise_setting("sn,sab->nab", onehot_wide, sequence_adapter)

    rows_float = tokens.astype(jnp.float32)
    attn_gain_wide = attn_gain.astype(jnp.float32)
    mlp_gain_wide = mlp_gain.astype(jnp.float32)
    query_gain_wide = query_gain.astype(jnp.float32)
    key_gain_wide = key_gain.astype(jnp.float32)
    normed_local = norm_rows(rows_float, attn_gain_wide).astype(jnp.bfloat16)
    normed = lax.all_gather(normed_local, "tensor", axis=0, tiled=True)
    query_full, key_full, value_full, output_full, router_full = fetch_attention(
        query_weight, key_weight, value_weight, output_weight, router_weight
    )
    sequence_adapter_input = normed.reshape(SEQUENCES_PER_DATA, SEQUENCE_TOKENS, D)

    def project(weight, downward_product, upward):
        down_selected = select(onehot, downward_product).astype(jnp.bfloat16)
        up_sel = select(onehot, upward)
        middle_product = jnp.einsum(
            "zmp,zpo->zmo",
            sequence_adapter_input,
            down_selected,
            preferred_element_type=jnp.float32,
        )
        side_part = precise_setting("slr,sre->sle", middle_product, up_sel)
        return (
            matmul(normed, weight) + side_part.reshape(GROUP_TOK, weight.shape[1]),
            middle_product,
            down_selected,
            up_sel,
        )

    query_raw, query_mid, query_down, query_up = project(query_full, query_lower, query_raise)
    key_raw, key_mid, key_down, key_up = project(key_full, key_lower, key_raise)
    value_raw, value_mid, value_down, value_up = project(value_full, value_lower, value_raise)
    query_total, key_total = lax.psum(
        (jnp.sum(query_raw * query_raw, axis=1), jnp.sum(key_raw * key_raw, axis=1)), "tensor"
    )

    def prepare(raw_rows, row_total, gain_row):
        inverse = lax.rsqrt(row_total / D + EPSILON)
        heads_view = (raw_rows * inverse[:, None] * gain_row).reshape(
            GROUP_TOK, local_heads, HEAD_DIM
        )
        return rotate(heads_view, cosine_table, sine_table)

    def prepare_query(raw_rows, row_total):
        return prepare(raw_rows, row_total, query_gain_wide)

    def prepare_key(raw_rows, row_total):
        return prepare(raw_rows, row_total, key_gain_wide)

    queries = prepare_query(query_raw, query_total).astype(jnp.bfloat16)
    key_rows = prepare_key(key_raw, key_total).astype(jnp.bfloat16)
    value_rows = value_raw.astype(jnp.bfloat16).reshape(GROUP_TOK, local_heads, HEAD_DIM)
    seq_queries = queries.reshape(SEQUENCES_PER_DATA, SEQUENCE_TOKENS, local_heads, HEAD_DIM)
    seq_keys = key_rows.reshape(SEQUENCES_PER_DATA, SEQUENCE_TOKENS, local_heads, HEAD_DIM)
    seq_values = value_rows.reshape(SEQUENCES_PER_DATA, SEQUENCE_TOKENS, local_heads, HEAD_DIM)

    def block_scores(position):
        sequence = position // blocks
        portion = position % blocks
        these_queries = lax.dynamic_slice_in_dim(
            lax.dynamic_index_in_dim(seq_queries, sequence, 0, keepdims=False),
            portion * block_rows,
            block_rows,
            0,
        )
        these_keys = lax.dynamic_index_in_dim(seq_keys, sequence, 0, keepdims=False)
        these_values = lax.dynamic_index_in_dim(seq_values, sequence, 0, keepdims=False)
        scores = (
            jnp.einsum(
                "qhd,khd->hqk", these_queries, these_keys, preferred_element_type=jnp.float32
            )
            * scale_factor
        )
        query_pos = portion * block_rows + jnp.arange(block_rows, dtype=jnp.int32)
        allowed = jnp.arange(SEQUENCE_TOKENS, dtype=jnp.int32)[None, :] <= query_pos[:, None]
        scores = jnp.where(allowed[None, :, :], scores, MASKED)
        return (scores, these_queries, these_keys, these_values, sequence, portion)

    def forward_block(position):
        scores, these_queries, these_keys, these_values, sequence, portion = block_scores(position)
        row_top = jnp.max(scores, axis=-1, keepdims=True)
        exponent = jnp.exp(scores - row_top)
        row_sum = jnp.sum(exponent, axis=-1, keepdims=True)
        soft_low = (exponent / row_sum).astype(jnp.bfloat16)
        attended_block = jnp.einsum(
            "hqk,khd->qhd", soft_low, these_values, preferred_element_type=jnp.float32
        )
        return (attended_block, (row_top + jnp.log(row_sum))[:, :, 0])

    attended_blocks, log_sums = lax.map(forward_block, positions)
    attention_result = attended_blocks.reshape(GROUP_TOK, width_local_shard).astype(jnp.bfloat16)
    output_downward = select(onehot, output_lower).astype(jnp.bfloat16)
    out_up = select(onehot, output_raise)
    out_mid = jnp.einsum(
        "zmp,zpo->zmo",
        attention_result.reshape(SEQUENCES_PER_DATA, SEQUENCE_TOKENS, width_local_shard),
        output_downward,
        preferred_element_type=jnp.float32,
    )
    out_side = precise_setting("slr,sre->sle", out_mid, out_up).reshape(GROUP_TOK, D)
    attn_out = lax.psum_scatter(
        (matmul(attention_result, output_full) + out_side).astype(jnp.bfloat16),
        "tensor",
        scatter_dimension=0,
        tiled=True,
    ).astype(jnp.float32)
    hidden_one = rows_float + attn_out
    normed_two_local = norm_rows(hidden_one, mlp_gain_wide).astype(jnp.bfloat16)
    normed_two, cotangent_full = (
        lax.all_gather(normed_two_local, "tensor", axis=0, tiled=True),
        lax.all_gather(out_cotangent, "tensor", axis=0, tiled=True),
    )
    route_prob = jax.nn.softmax(matmul(normed_two, router_full), axis=-1)
    route_mask = jnp.sum(
        (routes[:, :, None] == jnp.arange(EXPERTS, dtype=jnp.int32)[None, None, :]).astype(
            jnp.float32
        ),
        axis=1,
    )
    column_weight = jnp.transpose(route_prob * route_mask)
    column_mask = jnp.transpose(route_mask)
    grads_all = cotangent_full.astype(jnp.float32)

    def expert_forward(running, expert_gate, expert_up, expert_down, row_scale):
        gate_val = matmul(normed_two, expert_gate)
        up_val = matmul(normed_two, expert_up)
        activated = (jax.nn.silu(gate_val) * up_val).astype(jnp.bfloat16)
        expert_out = matmul(activated, expert_down)
        running = running + row_scale[:, None] * expert_out
        slot_grad = jnp.sum(grads_all * expert_out, axis=1)
        return (running, slot_grad, gate_val, up_val)

    def expert_backward(back_sum, expert_gate, expert_up, expert_down, row_scale, gate_val, up_val):
        sigmoid_gate = jax.nn.sigmoid(gate_val)
        silu_gate = gate_val * sigmoid_gate
        out_grad = (row_scale[:, None] * grads_all).astype(jnp.bfloat16)
        inner_grad = matmul_back(out_grad, expert_down)
        gate_grad = (
            inner_grad * up_val * sigmoid_gate * (1.0 + gate_val * (1.0 - sigmoid_gate))
        ).astype(jnp.bfloat16)
        up_grad = (inner_grad * silu_gate).astype(jnp.bfloat16)
        row_grad = matmul_back(gate_grad, expert_gate) + matmul_back(up_grad, expert_up)
        return back_sum + row_grad

    gate_all, up_all, down_all = (
        lax.all_gather(gate_weight, "dp", axis=1, tiled=True),
        lax.all_gather(up_weight, "dp", axis=1, tiled=True),
        lax.all_gather(down_weight, "dp", axis=2, tiled=True),
    )
    weight_source = (gate_all, up_all, down_all)

    def fetch_expert(gate_piece, up_piece, down_piece):
        return (gate_piece, up_piece, down_piece)

    zero_rows = jnp.zeros((GROUP_TOK, D), jnp.float32)

    def expert_step(carry_pair, item_set):
        gate_piece, up_piece, down_piece, row_scale = item_set
        expert_gate, expert_up, expert_down = fetch_expert(gate_piece, up_piece, down_piece)
        running, back_sum = carry_pair
        running, slot_grad, gate_val, up_val = expert_forward(
            running, expert_gate, expert_up, expert_down, row_scale
        )
        back_sum = expert_backward(
            back_sum, expert_gate, expert_up, expert_down, row_scale, gate_val, up_val
        )
        return ((running, back_sum), slot_grad)

    (moe_sum, back_sum), slot_grads = lax.scan(
        expert_step, (zero_rows, zero_rows), weight_source + (column_weight,)
    )
    moe_local = lax.psum_scatter(
        moe_sum.astype(jnp.bfloat16), "tensor", scatter_dimension=0, tiled=True
    ).astype(jnp.float32)
    normed_two_grad = lax.psum_scatter(
        back_sum.astype(jnp.bfloat16), "tensor", scatter_dimension=0, tiled=True
    ).astype(jnp.float32)
    prob_local_grad = lax.psum_scatter(
        jnp.transpose(slot_grads * column_mask).astype(jnp.bfloat16),
        "tensor",
        scatter_dimension=0,
        tiled=True,
    ).astype(jnp.float32)
    block_out = (hidden_one + moe_local).astype(jnp.bfloat16)
    prob_local = lax.dynamic_slice_in_dim(route_prob, first_row, local_rows, 0)
    logit_grad = (
        prob_local
        * (prob_local_grad - jnp.sum(prob_local * prob_local_grad, axis=1, keepdims=True))
    ).astype(jnp.bfloat16)
    normed_two_grad = normed_two_grad + matmul_back(logit_grad, router_full)

    def second_norm(values):
        return norm_rows(values, mlp_gain_wide)

    _, second_pull = jax.vjp(second_norm, hidden_one)
    hidden_grad = out_cotangent.astype(jnp.float32) + second_pull(normed_two_grad)[0]
    attn_grad = lax.all_gather(hidden_grad.astype(jnp.bfloat16), "tensor", axis=0, tiled=True)
    query_full, key_full, value_full, output_full, router_full = fetch_attention(
        query_weight, key_weight, value_weight, output_weight, router_weight
    )
    seq_grad = attn_grad.reshape(SEQUENCES_PER_DATA, SEQUENCE_TOKENS, D)
    output_middle_gradient = jnp.einsum(
        "sle,sre->slr", seq_grad, out_up.astype(jnp.bfloat16), preferred_element_type=jnp.float32
    )
    attended_grad = matmul_back(attn_grad, output_full) + precise_setting(
        "nkp,nbp->nkb", output_middle_gradient, output_downward.astype(jnp.float32)
    ).reshape(GROUP_TOK, width_local_shard)
    attended_grad = attended_grad.astype(jnp.bfloat16)
    grad_out_lower = precise_setting(
        "owb,owa->oba",
        attention_result.astype(jnp.float32).reshape(
            SEQUENCES_PER_DATA, SEQUENCE_TOKENS, width_local_shard
        ),
        output_middle_gradient,
    )
    grad_out_raise = precise_setting("slr,sle->sre", out_mid, seq_grad.astype(jnp.float32))
    seq_attended_grad = attended_grad.reshape(
        SEQUENCES_PER_DATA, SEQUENCE_TOKENS, local_heads, HEAD_DIM
    )

    def backward_block(position):
        scores, these_queries, these_keys, these_values, sequence, portion = block_scores(position)
        these_grads = lax.dynamic_slice_in_dim(
            lax.dynamic_index_in_dim(seq_attended_grad, sequence, 0, keepdims=False),
            portion * block_rows,
            block_rows,
            0,
        )
        log_sum = lax.dynamic_index_in_dim(log_sums, position, 0, keepdims=False)
        soft_rows = jnp.exp(scores - log_sum[:, :, None])
        value_part = jnp.einsum(
            "hqk,qhd->khd",
            soft_rows.astype(jnp.bfloat16),
            these_grads,
            preferred_element_type=jnp.float32,
        )
        soft_grad = jnp.einsum(
            "qhd,khd->hqk", these_grads, these_values, preferred_element_type=jnp.float32
        )
        score_grad = (
            soft_rows * (soft_grad - jnp.sum(soft_rows * soft_grad, axis=-1, keepdims=True))
        ).astype(jnp.bfloat16)
        query_part = (
            jnp.einsum("hqk,khd->qhd", score_grad, these_keys, preferred_element_type=jnp.float32)
            * scale_factor
        )
        key_part = (
            jnp.einsum(
                "hqk,qhd->khd", score_grad, these_queries, preferred_element_type=jnp.float32
            )
            * scale_factor
        )
        return (query_part, key_part, value_part)

    query_parts, key_parts, value_parts = lax.map(backward_block, positions)
    query_grad = query_parts.reshape(GROUP_TOK, local_heads, HEAD_DIM)
    key_grad = jnp.sum(
        key_parts.reshape(SEQUENCES_PER_DATA, blocks, SEQUENCE_TOKENS, local_heads, HEAD_DIM),
        axis=1,
    ).reshape(GROUP_TOK, local_heads, HEAD_DIM)
    value_grad = jnp.sum(
        value_parts.reshape(SEQUENCES_PER_DATA, blocks, SEQUENCE_TOKENS, local_heads, HEAD_DIM),
        axis=1,
    ).reshape(GROUP_TOK, width_local_shard)
    _, query_pull = jax.vjp(prepare_query, query_raw, query_total)
    query_direct, query_total_grad = query_pull(query_grad)
    _, key_pull = jax.vjp(prepare_key, key_raw, key_total)
    key_direct, key_total_grad = key_pull(key_grad)
    query_sum_grad, key_sum_grad = lax.psum((query_total_grad, key_total_grad), "tensor")
    query_raw_grad = (query_direct + 2.0 * query_raw * query_sum_grad[:, None]).astype(jnp.bfloat16)
    key_raw_grad = (key_direct + 2.0 * key_raw * key_sum_grad[:, None]).astype(jnp.bfloat16)
    value_raw_grad = value_grad.astype(jnp.bfloat16)
    normed_broadcast = normed.astype(jnp.float32).reshape(SEQUENCES_PER_DATA, SEQUENCE_TOKENS, D)

    def project_back(raw_grad, weight, middle_product, down_selected, up_sel):
        seq_raw = raw_grad.reshape(SEQUENCES_PER_DATA, SEQUENCE_TOKENS, width_local_shard)
        middle_gradient = jnp.einsum(
            "sle,sre->slr", seq_raw, up_sel.astype(jnp.bfloat16), preferred_element_type=jnp.float32
        )
        grad_upward = precise_setting("slr,sle->sre", middle_product, seq_raw.astype(jnp.float32))
        downward_gradient = precise_setting("owb,owa->oba", normed_broadcast, middle_gradient)
        input_part = matmul_back(raw_grad, weight) + precise_setting(
            "nkp,nbp->nkb", middle_gradient, down_selected.astype(jnp.float32)
        ).reshape(GROUP_TOK, D)
        return (input_part, grad_upward, downward_gradient)

    query_in, query_up_grad, query_down_grad = project_back(
        query_raw_grad, query_full, query_mid, query_down, query_up
    )
    key_in, key_up_grad, key_down_grad = project_back(
        key_raw_grad, key_full, key_mid, key_down, key_up
    )
    value_in, value_up_grad, value_down_grad = project_back(
        value_raw_grad, value_full, value_mid, value_down, value_up
    )
    normed_grad = lax.psum_scatter(
        (query_in + key_in + value_in).astype(jnp.bfloat16),
        "tensor",
        scatter_dimension=0,
        tiled=True,
    ).astype(jnp.float32)

    def first_norm(values):
        return norm_rows(values, attn_gain_wide)

    _, first_pull = jax.vjp(first_norm, rows_float)
    input_grad = (hidden_grad + first_pull(normed_grad)[0]).astype(jnp.bfloat16)
    split_sums = (
        lax.psum(spread(query_up_grad).astype(jnp.bfloat16), "dp").astype(jnp.float32),
        lax.psum(spread(key_up_grad).astype(jnp.bfloat16), "dp").astype(jnp.float32),
        lax.psum(spread(value_up_grad).astype(jnp.bfloat16), "dp").astype(jnp.float32),
        lax.psum(spread(grad_out_lower).astype(jnp.bfloat16), "dp").astype(jnp.float32),
    )
    full_sums = lax.psum(
        (
            spread(query_down_grad),
            spread(key_down_grad),
            spread(value_down_grad),
            spread(grad_out_raise),
        ),
        ("dp", "tensor"),
    )
    return (
        block_out,
        input_grad,
        full_sums[0],
        split_sums[0],
        full_sums[1],
        split_sums[1],
        full_sums[2],
        split_sums[2],
        split_sums[3],
        full_sums[3],
    )


def solution(mesh):
    in_specs = (
        P(("dp", "tensor"), None),
        P(),
        P("tensor"),
        P("tensor"),
        P("dp", "tensor"),
        P("dp", "tensor"),
        P("dp", "tensor"),
        P("tensor", "dp"),
        P(),
        P("dp", None),
        P(None, "dp", "tensor"),
        P(None, "dp", "tensor"),
        P(None, "tensor", "dp"),
        P(),
        P(None, None, "tensor"),
        P(),
        P(None, None, "tensor"),
        P(),
        P(None, None, "tensor"),
        P(None, "tensor", None),
        P(),
        P("dp", None),
        P("dp"),
        P(("dp", "tensor"), None),
    )
    out_specs = (
        P(("dp", "tensor"), None),
        P(("dp", "tensor"), None),
        P(),
        P(None, None, "tensor"),
        P(),
        P(None, None, "tensor"),
        P(),
        P(None, None, "tensor"),
        P(None, "tensor", None),
        P(),
    )
    return jax.shard_map(
        per_device, mesh=mesh, in_specs=in_specs, out_specs=out_specs, check_vma=False
    )
```

profile of v0, /device:TPU:0, one launch (start us, length us, event | category | flops | bytes accessed | tf_op | source)
XLA Modules:
  0.0 2038.5 jit_solution(18312440384582110385)
XLA Ops:
  22.2 74.2 %all-gather.12.cloned.1.call-done = bf16[1024,2048]{1,0:T(8,128)(2,1)} async-done(((bf16[256,2048]{1,0:T(8,128)(2,1)}), bf16[1024,2048]{1,0:T(8,128)(2,1)}) %all-gather.12.cloned.1.call-update) | async-done | bytes 4194320 | tf_op jit(solution)/shard_map/all_gather | solution.py:123
  99.8 25.0 %all-gather.14.cloned.1.call-done = bf16[2048,512]{1,0:T(8,128)(2,1)} async-done(((bf16[256,512]{1,0:T(8,128)(2,1)}), bf16[2048,512]{1,0:T(8,128)(2,1)}) %all-gather.14.cloned.1.call-update) | async-done | bytes 2097168 | tf_op jit(solution)/shard_map/all_gather | solution.py:66
  135.1 19.5 all-gather.16.cloned.1.call-done
  163.0 12.0 all-reduce.6
  198.0 21.7 %while.45 = (s32[]{:T(128)}, bf16[2,512,4,128]{3,1,2,0:T(8,128)(2,1)}, f32[2,4,512]{2,1,0:T(4,128)S(1)}, s32[2]{0:T(128)S(1)}, bf16[1,1024,4,128]{3,1,2,0:T(8,12...) while((s32[]{:T(128)}, ...), condition=%wide.region_8.9_spmd, body=%wide.region_5.8_spmd.sunk | while | flops 1099430400 | bytes 35197764 | solution.py:206
  237.6 73.6 %reduce-scatter.6.cloned.1.call-done = bf16[256,2048]{1,0:T(8,128)(2,1)} async-done(((bf16[1024,2048]{1,0:T(8,128)(2,1)}), bf16[256,2048]{1,0:T(8,128)(2,1)}) %reduce-scatter.6.cloned.1.call-update) | async-done | bytes 1048592 | tf_op jit(solution)/shard_map/reduce_scatter | solution.py:217
  327.9 66.3 %all-gather.30.cloned.1.call-done = bf16[1024,2048]{1,0:T(8,128)(2,1)} async-done(((bf16[256,2048]{1,0:T(8,128)(2,1)}), bf16[1024,2048]{1,0:T(8,128)(2,1)}) %all-gather.30.cloned.1.call-update) | async-done | bytes 4194320 | tf_op jit(solution)/shard_map/all_gather | solution.py:227
  400.8 75.0 %all-gather.22.cloned.1.call-done = bf16[1024,2048]{1,0:T(8,128)(2,1)} async-done(((bf16[256,2048]{1,0:T(8,128)(2,1)}), bf16[1024,2048]{1,0:T(8,128)(2,1)}) %all-gather.22.cloned.1.call-update) | async-done | bytes 4194320 | tf_op jit(solution)/shard_map/all_gather | solution.py:226
  479.2 87.0 %all-gather.24.cloned.1.call-done = bf16[16,2048,256]{2,1,0:T(8,128)(2,1)} async-done(((bf16[16,256,256]{2,1,0:T(8,128)(2,1)}), bf16[16,2048,256]{2,1,0:T(8,128)(2,1)}) %all-gather.24.cloned.1.call-update) | async-done | bytes 16777232 | tf_op jit(solution)/shard_map/all_gather | solution.py:262
  566.2 91.8 %all-gather.26.cloned.1.call-done = bf16[16,2048,256]{2,1,0:T(8,128)(2,1)} async-done(((bf16[16,256,256]{2,1,0:T(8,128)(2,1)}), bf16[16,2048,256]{2,1,0:T(8,128)(2,1)}) %all-gather.26.cloned.1.call-update) | async-done | bytes 16777232 | tf_op jit(solution)/shard_map/all_gather | solution.py:263
  658.0 95.2 %all-gather.28.cloned.1.call-done = bf16[16,256,2048]{2,1,0:T(8,128)(2,1)} async-done(((bf16[16,256,256]{2,1,0:T(8,128)(2,1)}), bf16[16,256,2048]{2,1,0:T(8,128)(2,1)}) %all-gather.28.cloned.1.call-update) | async-done | bytes 16777232 | tf_op jit(solution)/shard_map/all_gather | solution.py:264
  753.2 609.6 %while.47 = (s32[]{:T(128)}, f32[1024,2048]{1,0:T(8,128)}, f32[1024,2048]{1,0:T(8,128)}, f32[16,1024]{1,0:T(8,128)S(1)}, f32[16,1024]{1,0:T(8,128)S(1)}, /*index...) while((s32[]{:T(128)}, f32[1024,2048]{1,0:T(8,128)}, ...), condition=%wide.region_16.17_spmd.clone, body=%wide.region_14.16_spmd.clone.sunk | while | flops 6469188608 | bytes 117472472 | solution.py:285
  842.7 11.1 select_add_fusion.3
  881.1 11.1 select_add_fusion.3
  919.5 11.1 select_add_fusion.3
  957.9 11.1 select_add_fusion.3
  996.3 11.1 select_add_fusion.3
  1034.7 11.1 select_add_fusion.3
  1073.1 11.1 select_add_fusion.3
  1111.5 11.1 select_add_fusion.3
  1149.9 11.1 select_add_fusion.3
  1188.3 11.1 select_add_fusion.3
  1226.7 11.1 select_add_fusion.3
  1265.1 11.1 select_add_fusion.3
  1369.8 12.7 reduce-scatter.12.cloned.1.call-done
  1383.3 76.6 %reduce-scatter.10.cloned.1.call-done = bf16[256,2048]{1,0:T(8,128)(2,1)} async-done(((bf16[1024,2048]{1,0:T(8,128)(2,1)}), bf16[256,2048]{1,0:T(8,128)(2,1)}) %reduce-scatter.10.cloned.1.call-update) | async-done | bytes 1048592 | tf_op jit(solution)/shard_map/reduce_scatter | solution.py:291
  1466.6 80.9 %all-gather.32.cloned.1.call-done = bf16[1024,2048]{1,0:T(8,128)(2,1)} async-done(((bf16[256,2048]{1,0:T(8,128)(2,1)}), bf16[1024,2048]{1,0:T(8,128)(2,1)}) %all-gather.32.cloned.1.call-update) | async-done | bytes 4194320 | tf_op jit(solution)/shard_map/all_gather | solution.py:313
  1557.7 53.7 %while.46 = (s32[]{:T(128)}, f32[2,512,4,128]{3,1,0,2:T(8,128)}, f32[2,1024,4,128]{1,3,2,0:T(8,128)}, f32[2,1024,4,128]{1,3,2,0:T(8,128)}, s32[2]{0:T(128)S(1)},...) while((s32[]{:T(128)}, f32[2,512,4,128]{3,1,0,2:T(8,128)}, ...), condition=%wide.region_24.25_spmd, body=%wide.region_22.24_spmd.sunk | while | flops 2717121024 | bytes 155251760 | solution.py:371
  1681.3 17.9 add_convert_fusion
  1724.6 69.9 %reduce-scatter.14.cloned.1.call-done = bf16[256,2048]{1,0:T(8,128)(2,1)} async-done(((bf16[1024,2048]{1,0:T(8,128)(2,1)}), bf16[256,2048]{1,0:T(8,128)(2,1)}) %reduce-scatter.14.cloned.1.call-update) | async-done | bytes 1048592 | tf_op jit(solution)/shard_map/reduce_scatter | solution.py:412
  1796.2 77.9 %reduce-scatter.8.cloned.1.call-done = bf16[256,2048]{1,0:T(8,128)(2,1)} async-done(((bf16[1024,2048]{1,0:T(8,128)(2,1)}), bf16[256,2048]{1,0:T(8,128)(2,1)}) %reduce-scatter.8.cloned.1.call-update) | async-done | bytes 1048592 | tf_op jit(solution)/shard_map/reduce_scatter | solution.py:288
  1879.4 145.1 %all-reduce.11.cloned.1.call-done = (f32[8,2048,16]{1,2,0:T(8,128)}, f32[8,2048,16]{1,2,0:T(8,128)}, f32[8,2048,16]{1,2,0:T(8,128)}, f32[8,16,2048]{2,1,0:T(8,128)}) async-done(((f32[8,2048,16]{1,2,0:T(8,128)}, f32[8,2048,16]{1,2,0:T(8,128)}, f32[8,2048,16]{1,2,0:T(8,128)}, f32[8,16,2048]{2,1,0:T(8,128)}), (f32[8,2048,16]{1,2,0:T(8,128)}, f32[8,2048,16]{1,2,0:T(8,128)}, f32[8,2048,16]{1,2,0:T(8,128)}, ...) | async-done | bytes 4194320 | tf_op jit(solution)/shard_map/psum | solution.py:430
  (647 shorter events, 776.0 us)
Async XLA Ops:
  7.2 89.2 %all-gather.12.cloned.1.call-start = ((), (), s32[]{:S(2)}) async-start(), calls=%async_computation.5 | async-start | bytes 5242880 | tf_op jit(solution)/shard_map/all_gather | solution.py:123
  12.8 112.0 %all-gather.14.cloned.1.call-start = ((), (), s32[]{:S(2)}) async-start(), calls=%async_computation.6 | async-start | bytes 2359296 | tf_op jit(solution)/shard_map/all_gather | solution.py:66
  13.6 141.1 %all-gather.16.cloned.1.call-start = ((), (), s32[]{:S(2)}) async-start(), calls=%async_computation.7 | async-start | bytes 2359296 | tf_op jit(solution)/shard_map/all_gather | solution.py:67
  14.3 173.3 %all-gather.18.cloned.1.call-start = ((), (), s32[]{:S(2)}) async-start(), calls=%async_computation.8 | async-start | bytes 2359296 | tf_op jit(solution)/shard_map/all_gather | solution.py:68
  14.9 209.1 %all-gather.20.cloned.1.call-start = ((), (), s32[]{:S(2)}) async-start(), calls=%async_computation.9 | async-start | bytes 2359296 | tf_op jit(solution)/shard_map/all_gather | solution.py:69
  15.5 295.8 %reduce-scatter.6.cloned.1.call-start = ((), (), s32[]{:S(2)}) async-start(), calls=%async_computation.10 | async-start | bytes 5242880 | tf_op jit(solution)/shard_map/reduce_scatter | solution.py:217
  17.7 116.2 %copy-start.41 = (bf16[1,2048,16]{2,1,0:T(8,128)(2,1)}, bf16[1,2048,16]{2,1,0:T(8,128)(2,1)S(1)}, u32[]{:S(2)}) copy-start(bf16[1,2048,16]{2,1,0:T(8,128)(2,1)S(1)} %copy.103) | copy-start | bytes 196612
  19.7 164.5 %copy-start.37 = (bf16[1,2048,16]{2,1,0:T(8,128)(2,1)}, bf16[1,2048,16]{2,1,0:T(8,128)(2,1)S(1)}, u32[]{:S(2)}) copy-start(bf16[1,2048,16]{2,1,0:T(8,128)(2,1)S(1)} %copy.107) | copy-start | bytes 196612
  20.0 202.6 %copy-start.50 = (bf16[1,512,16]{2,1,0:T(8,128)(2,1)}, bf16[1,512,16]{2,1,0:T(8,128)(2,1)S(1)}, u32[]{:S(2)}) copy-start(bf16[1,512,16]{2,1,0:T(8,128)(2,1)S(1)} %copy.111) | copy-start | bytes 49156
  20.2 109.8 %copy-start.71 = (f32[1,16,512]{2,0,1:T(1,128)}, f32[1,16,512]{2,0,1:T(1,128)S(1)}, u32[]{:S(2)}) copy-start(f32[1,16,512]{2,0,1:T(1,128)S(1)} %fusion.113) | copy-start | bytes 98308
  20.5 139.4 %copy-start.69 = (f32[1,16,512]{2,0,1:T(1,128)}, f32[1,16,512]{2,0,1:T(1,128)S(1)}, u32[]{:S(2)}) copy-start(f32[1,16,512]{2,0,1:T(1,128)S(1)} %fusion.111) | copy-start | bytes 98308
  21.5 156.2 %copy-start.45 = (f32[1024,64]{0,1:T(8,128)}, f32[1024,64]{0,1:T(8,128)S(1)}, u32[]{:S(2)}) copy-start(f32[1024,64]{0,1:T(8,128)S(1)} %get-tuple-element.482) | copy-start | bytes 786436
  21.5 156.2 %copy-start.47 = (f32[1024,64]{0,1:T(8,128)}, f32[1024,64]{0,1:T(8,128)S(1)}, u32[]{:S(2)}) copy-start(f32[1024,64]{0,1:T(8,128)S(1)} %get-tuple-element.483) | copy-start | bytes 786436
  21.7 171.2 %copy-start.67 = (f32[1,16,512]{2,0,1:T(1,128)}, f32[1,16,512]{2,0,1:T(1,128)S(1)}, u32[]{:S(2)}) copy-start(f32[1,16,512]{2,0,1:T(1,128)S(1)} %fusion.109) | copy-start | bytes 98308
  22.2 206.1 %copy-start.60 = (f32[1,16,2048]{2,0,1:T(1,128)}, f32[1,16,2048]{2,0,1:T(1,128)S(1)}, u32[]{:S(2)}) copy-start(f32[1,16,2048]{2,0,1:T(1,128)S(1)} %fusion.93) | copy-start | bytes 393220
  236.8 157.4 %all-gather.30.cloned.1.call-start = ((), (), s32[]{:S(2)}) async-start(), calls=%async_computation.15 | async-start | bytes 5242880 | tf_op jit(solution)/shard_map/all_gather | solution.py:227
  237.6 238.2 %all-gather.22.cloned.1.call-start = ((), (), s32[]{:S(2)}) async-start(), calls=%async_computation.11 | async-start | bytes 5242880 | tf_op jit(solution)/shard_map/all_gather | solution.py:226
  316.6 249.6 %all-gather.24.cloned.1.call-start = ((), (), s32[]{:S(2)}) async-start(), calls=%async_computation.12 | async-start | bytes 18874368 | tf_op jit(solution)/shard_map/all_gather | solution.py:262
  317.4 340.6 %all-gather.26.cloned.1.call-start = ((), (), s32[]{:S(2)}) async-start(), calls=%async_computation.13 | async-start | bytes 18874368 | tf_op jit(solution)/shard_map/all_gather | solution.py:263
  318.0 435.2 %all-gather.28.cloned.1.call-start = ((), (), s32[]{:S(2)}) async-start(), calls=%async_computation.14 | async-start | bytes 18874368 | tf_op jit(solution)/shard_map/all_gather | solution.py:264
  318.7 1063.8 %reduce-scatter.12.cloned.1.call-start = ((), (), s32[]{:S(2)}) async-start(), calls=%async_computation.18 | async-start | bytes 40960 | tf_op jit(solution)/shard_map/reduce_scatter | solution.py:294
  1363.5 96.3 %reduce-scatter.10.cloned.1.call-start = ((), (), s32[]{:S(2)}) async-start(), calls=%async_computation.17 | async-start | bytes 5242880 | tf_op jit(solution)/shard_map/reduce_scatter | solution.py:291
  1369.7 93.4 %copy-start.92 = (f32[256]{0:T(256)S(1)}, f32[256]{0:T(256)}, u32[]{:S(2)}) copy-start(f32[256]{0:T(256)} %copy-done.91) | copy-start | bytes 3076
  1369.8 177.7 %all-gather.32.cloned.1.call-start = ((), (), s32[]{:S(2)}) async-start(), calls=%async_computation.19 | async-start | bytes 5242880 | tf_op jit(solution)/shard_map/all_gather | solution.py:313
  1466.1 251.9 %all-reduce.13.cloned.1.call-start = ((), (), s32[]{:S(2)}) async-start(), calls=%async_computation.22 | async-start | bytes 1048576 | tf_op jit(solution)/shard_map/psum | solution.py:425
  1662.2 132.4 %reduce-scatter.14.cloned.1.call-start = ((), (), s32[]{:S(2)}) async-start(), calls=%async_computation.20 | async-start | bytes 5242880 | tf_op jit(solution)/shard_map/reduce_scatter | solution.py:412
  1699.2 174.9 %reduce-scatter.8.cloned.1.call-start = ((), (), s32[]{:S(2)}) async-start(), calls=%async_computation.16 | async-start | bytes 5242880 | tf_op jit(solution)/shard_map/reduce_scatter | solution.py:288
  1705.2 319.2 %all-reduce.11.cloned.1.call-start = ((), (), s32[]{:S(2)}) async-start(), calls=%async_computation.21 | async-start | bytes 8388608 | tf_op jit(solution)/shard_map/psum | solution.py:430
  1717.9 156.2 %copy-start.18 = (bf16[256,2048]{1,0:T(8,128)(2,1)S(1)}, bf16[256,2048]{1,0:T(8,128)(2,1)}, u32[]{:S(2)}) copy-start(bf16[256,2048]{1,0:T(8,128)(2,1)} %reduce-scatter.6.cloned.1.call-done) | copy-start | bytes 3145732
  1717.9 156.2 %copy-start.93 = (f32[256]{0:T(256)S(1)}, f32[256]{0:T(256)}, u32[]{:S(2)}) copy-start(f32[256]{0:T(256)} %copy-done.91) | copy-start | bytes 3076
  1717.9 156.2 %copy-start.99 = (f32[256]{0:T(256)S(1)}, f32[256]{0:T(256)}, u32[]{:S(2)}) copy-start(f32[256]{0:T(256)} %copy-done.98) | copy-start | bytes 3076
  1717.9 156.2 %copy-start.101 = (f32[256]{0:T(256)S(1)}, f32[256]{0:T(256)}, u32[]{:S(2)}) copy-start(f32[256]{0:T(256)} %copy-done.100) | copy-start | bytes 3076
  (153 other events, 1816.5 us)
Sparse Core Ops, SparseCore 0:
  12.9 83.4 all-gather.11
  98.3 26.4 all-gather.13
  126.7 27.8 all-gather.15
  156.4 27.8 all-gather.17
  186.0 28.1 all-gather.19
  236.9 74.2 reduce-scatter.5
  312.9 81.2 all-gather.29
  396.4 79.2 all-gather.21
  477.8 88.3 all-gather.23
  568.1 89.8 all-gather.25
  660.1 93.1 all-gather.27
  1363.6 18.8 reduce-scatter.11
  1384.8 74.9 reduce-scatter.9
  1466.2 81.2 all-gather.31
  1662.3 53.9 all-reduce.12
  1718.4 76.1 reduce-scatter.13
  1796.8 77.2 reduce-scatter.7
  1881.0 143.4 all-reduce.10
where the time goes:
time: 2050 us; the launch traced here: 2040 us
  waiting for transfers between devices  1080 us (53%)
  matrix products  764 us (37%)
  other arithmetic  81.6 us (4%)
  local copies, waits for them, and re-layouts  56.2 us (3%)
  blocking collectives  30.1 us (1%)
    dot_general x53, matrix products, matmul_back(): lax.dot_general(left, right, (((1,), (1,)), ((), ())), preferred_element_...  381 us
    dot_general x53, matrix products, matmul(): return jnp.dot(left, right, preferred_element_type=jnp.float32)  258 us
    psum x1, waiting for transfers between devices, per_device(): lax.psum((spread(query_down_grad), spread(key_down_grad), spread(value_do...  145 us
    all_gather x1, waiting for transfers between devices, per_device(): lax.all_gather(down_weight, 'dp', axis=2, tiled=True)  95.2 us
    all_gather x1, waiting for transfers between devices, per_device(): lax.all_gather(up_weight, 'dp', axis=1, tiled=True)  91.8 us
    all_gather x1, waiting for transfers between devices, per_device(): lax.all_gather(gate_weight, 'dp', axis=1, tiled=True)  87 us
    all_gather x1, waiting for transfers between devices, per_device(): lax.all_gather(hidden_grad.astype(jnp.bfloat16), 'tensor', axis=0, tiled=...  80.9 us
    reduce_scatter x1, waiting for transfers between devices, per_device(): lax.psum_scatter(moe_sum.astype(jnp.bfloat16), 'tensor', scatter_dimensio...  77.9 us
  transfers between devices with their start and end apart: 18, of which 15 were waited for; matrix products, arithmetic and copies ran while one was open for 8% of the time, Pallas kernels for 0%

commit v1 on v0

v1 whole, which is shorter than its diff:
```python
import functools

import jax
import jax.numpy as jnp
from jax import lax
from jax.experimental import pallas as pl
from jax.experimental.pallas import tpu as pltpu
from jax.sharding import PartitionSpec as P

HEAD_DIM = 128
EPSILON = 1e-05
ROPE_BASE = 10000.0
MASKED = -1e30
MIB = 1024 * 1024

f32 = jnp.float32
bf16 = jnp.bfloat16


def nn(left, right):
    return jnp.dot(left, right, preferred_element_type=f32)


def nt(left, right):
    return lax.dot_general(left, right, (((1,), (1,)), ((), ())), preferred_element_type=f32)


def tn(left, right):
    return lax.dot_general(left, right, (((0,), (0,)), ((), ())), preferred_element_type=f32)


def after(value, *others):
    return lax.optimization_barrier((value,) + others)[0]


def line_gather(unit, axis, count):
    me = lax.axis_index(axis)
    rows = unit.shape[0]
    rights, lefts = [unit], [unit]
    for step in range(1, count):
        rights.append(
            lax.ppermute(rights[-1], axis, [(i, i + 1) for i in range(step - 1, count - 1)])
        )
        lefts.append(
            lax.ppermute(lefts[-1], axis, [(i, i - 1) for i in range(1, count - step + 1)])
        )
    whole = jnp.zeros((count * rows,) + unit.shape[1:], unit.dtype)
    whole = lax.dynamic_update_slice_in_dim(whole, unit, me * rows, 0)
    for step in range(1, count):
        piece = jnp.where(me >= step, rights[step], lefts[count - step])
        place = lax.rem(me - step + count, count)
        whole = lax.dynamic_update_slice_in_dim(whole, piece, place * rows, 0)
    return whole


def line_scatter(parts, axis, count):
    me = lax.axis_index(axis)
    rows = parts.shape[0] // count

    def own(index):
        return lax.dynamic_slice_in_dim(parts, index * rows, rows, 0).astype(f32)

    right = left = None
    for step in range(1, count):
        to_right = own(jnp.clip(count - step + me, 0, count - 1))
        to_left = own(jnp.clip(me + step - count, 0, count - 1))
        if right is not None:
            to_right = to_right + right.astype(f32)
            to_left = to_left + left.astype(f32)
        right = lax.ppermute(
            to_right.astype(bf16), axis, [(i, i + 1) for i in range(min(step, count - 1))]
        )
        left = lax.ppermute(
            to_left.astype(bf16),
            axis,
            [(i, i - 1) for i in range(count - 1, max(count - 1 - step, 0), -1)],
        )
    return own(me) + right.astype(f32) + left.astype(f32)


def direct_scatter(parts, axis, count):
    me = lax.axis_index(axis)
    rows = parts.shape[0] // count
    total = lax.dynamic_slice_in_dim(parts, me * rows, rows, 0).astype(f32)
    for shift in range(1, count):
        target = lax.rem(me + shift, count)
        part = lax.dynamic_slice_in_dim(parts, target * rows, rows, 0)
        got = lax.ppermute(part, axis, [(i, (i + shift) % count) for i in range(count)])
        total = total + got.astype(f32)
    return total


def direct_sum(value, axis, count):
    total = value
    for shift in range(1, count):
        total = total + lax.ppermute(
            value, axis, [(i, (i + shift) % count) for i in range(count)]
        )
    return total


def rope_tables(row_count):
    position = jnp.arange(row_count, dtype=jnp.int32).astype(f32)
    half = HEAD_DIM // 2
    frequency = ROPE_BASE ** (-2.0 * jnp.arange(half, dtype=f32) / HEAD_DIM)
    angles = position[:, None] * frequency[None, :]
    cosine, sine = jnp.cos(angles), jnp.sin(angles)
    return (
        jnp.concatenate([cosine, cosine], axis=1),
        jnp.concatenate([-sine, sine], axis=1),
    )


def causal_scores(q_block, keys, first):
    scores = nt(q_block, keys) * (HEAD_DIM**-0.5)
    rows = first + lax.broadcasted_iota(jnp.int32, scores.shape, 0)
    columns = lax.broadcasted_iota(jnp.int32, scores.shape, 1)
    return jnp.where(columns <= rows, scores, MASKED)


def attend_kernel(
    block,
    query_raw,
    key_raw,
    value_raw,
    query_inverse,
    key_inverse,
    query_gain,
    key_gain,
    cosine,
    sine,
    queries,
    keys,
    values,
    attended,
    log_sums,
):
    half = HEAD_DIM // 2
    rows = query_raw.shape[0]

    def rotated(raw, inverse, gain):
        head = raw[...] * inverse[...] * gain[...]
        return (head * cosine[...] + pltpu.roll(head, half, 1) * sine[...]).astype(bf16)

    queries[...] = rotated(query_raw, query_inverse, query_gain)
    keys[...] = rotated(key_raw, key_inverse, key_gain)
    values[...] = value_raw[...].astype(bf16)
    for first in range(0, rows, block):
        end = first + block
        here = slice(first, end)
        scores = causal_scores(queries[here, :], keys[0:end, :], first)
        top = jnp.max(scores, axis=1, keepdims=True)
        exponent = jnp.exp(scores - top)
        total = jnp.sum(exponent, axis=1, keepdims=True)
        soft = (exponent * (1.0 / total)).astype(bf16)
        attended[here, :] = nn(soft, values[0:end, :]).astype(bf16)
        log_sums[0, here, :] = top + jnp.log(total)


def attend(raws, inverses, gains, tables):
    rows, width = raws[0].shape
    heads = width // HEAD_DIM
    by_head = pl.BlockSpec((rows, HEAD_DIM), lambda h: (0, h))
    column = pl.BlockSpec((rows, 1), lambda h: (0, 0))
    gain = pl.BlockSpec((1, HEAD_DIM), lambda h: (0, h))
    table = pl.BlockSpec((rows, HEAD_DIM), lambda h: (0, 0))
    wide = jax.ShapeDtypeStruct((rows, width), bf16)
    return pl.pallas_call(
        functools.partial(attend_kernel, min(256, rows)),
        grid=(heads,),
        in_specs=[by_head] * 3 + [column] * 2 + [gain] * 2 + [table] * 2,
        out_specs=[by_head] * 4 + [pl.BlockSpec((1, rows, 1), lambda h: (h, 0, 0))],
        out_shape=[wide] * 4 + [jax.ShapeDtypeStruct((heads, rows, 1), f32)],
        compiler_params=pltpu.CompilerParams(vmem_limit_bytes=40 * MIB),
        cost_estimate=pl.CostEstimate(
            flops=2 * rows * rows * width,
            bytes_accessed=20 * rows * width,
            transcendentals=rows * rows * heads // 2,
        ),
    )(*raws, *inverses, *gains, *tables)


def attend_back_kernel(
    block,
    queries,
    keys,
    values,
    grads,
    log_sums,
    query_raw,
    key_raw,
    query_inverse,
    key_inverse,
    query_gain,
    key_gain,
    cosine,
    sine,
    query_out,
    key_out,
    value_out,
    query_dot,
    key_dot,
    query_grad,
    key_grad,
    value_grad,
):
    half = HEAD_DIM // 2
    rows = queries.shape[0]
    scale = HEAD_DIM**-0.5
    for first in range(rows - block, -1, -block):
        end = first + block
        here = slice(first, end)
        scores = causal_scores(queries[here, :], keys[0:end, :], first)
        soft = jnp.exp(scores - log_sums[0, here, :])
        soft_grad = nt(grads[here, :], values[0:end, :])
        inner = jnp.sum(soft * soft_grad, axis=1, keepdims=True)
        score_grad = (soft * (soft_grad - inner)).astype(bf16)
        value_part = tn(soft.astype(bf16), grads[here, :])
        key_part = tn(score_grad, queries[here, :])
        query_grad[here, :] = nn(score_grad, keys[0:end, :])
        if end == rows:
            value_grad[...] = value_part
            key_grad[...] = key_part
        else:
            value_grad[0:end, :] += value_part
            key_grad[0:end, :] += key_part

    def pulled(grad, raw, inverse, gain, out, dot):
        turned = grad[...] * scale
        turned = turned * cosine[...] - pltpu.roll(turned, half, 1) * sine[...]
        turned = turned * gain[...]
        out[...] = turned
        partial = jnp.sum(turned * (raw[...] * inverse[...]), axis=1, keepdims=True)

        @pl.when(pl.program_id(0) == 0)
        def _():
            dot[...] = partial

        @pl.when(pl.program_id(0) > 0)
        def _():
            dot[...] += partial

    pulled(query_grad, query_raw, query_inverse, query_gain, query_out, query_dot)
    pulled(key_grad, key_raw, key_inverse, key_gain, key_out, key_dot)
    value_out[...] = value_grad[...].astype(bf16)


def attend_back(heads_in, grads, log_sums, raws, inverses, gains, tables):
    rows, width = grads.shape
    heads = width // HEAD_DIM
    by_head = pl.BlockSpec((rows, HEAD_DIM), lambda h: (0, h))
    column = pl.BlockSpec((rows, 1), lambda h: (0, 0))
    gain = pl.BlockSpec((1, HEAD_DIM), lambda h: (0, h))
    table = pl.BlockSpec((rows, HEAD_DIM), lambda h: (0, 0))
    return pl.pallas_call(
        functools.partial(attend_back_kernel, min(256, rows)),
        grid=(heads,),
        in_specs=[by_head] * 4
        + [pl.BlockSpec((1, rows, 1), lambda h: (h, 0, 0))]
        + [by_head] * 2
        + [column] * 2
        + [gain] * 2
        + [table] * 2,
        out_specs=[by_head] * 3 + [column] * 2,
        out_shape=[
            jax.ShapeDtypeStruct((rows, width), f32),
            jax.ShapeDtypeStruct((rows, width), f32),
            jax.ShapeDtypeStruct((rows, width), bf16),
            jax.ShapeDtypeStruct((rows, 1), f32),
            jax.ShapeDtypeStruct((rows, 1), f32),
        ],
        scratch_shapes=[pltpu.VMEM((rows, HEAD_DIM), f32)] * 3,
        compiler_params=pltpu.CompilerParams(vmem_limit_bytes=40 * MIB),
        cost_estimate=pl.CostEstimate(
            flops=5 * rows * rows * width,
            bytes_accessed=28 * rows * width,
            transcendentals=rows * rows * heads // 2,
        ),
    )(*heads_in, grads, log_sums, *raws[:2], *inverses, *gains, *tables)


def experts_kernel(
    rows_in, grads, weight, gates, ups, downs, moe, back, slots, moe_sum, back_sum
):
    expert = pl.program_id(0)
    pieces, _, hidden, wide = downs.shape
    depth = pieces * wide
    gate_matrix = gates[:, 0].reshape(depth, hidden)
    up_matrix = ups[:, 0].reshape(depth, hidden)
    gate = nn(rows_in[...], gate_matrix)
    up = nn(rows_in[...], up_matrix)
    inner = nt(grads[:, 0:wide], downs[0, 0])
    for piece in range(1, pieces):
        inner += nt(grads[:, piece * wide : (piece + 1) * wide], downs[piece, 0])
    lane = lax.broadcasted_iota(jnp.int32, weight.shape, 1)
    row_scale = jnp.sum(jnp.where(lane == expert, weight[...], 0.0), axis=1, keepdims=True)
    sigmoid = jax.nn.sigmoid(gate)
    silu = gate * sigmoid
    activated = (silu * up).astype(bf16).astype(f32)
    slot = jnp.sum(activated * inner, axis=1, keepdims=True)
    scaled = (row_scale * activated).astype(bf16)
    inner = row_scale * inner
    gate_grad = (inner * up * (sigmoid * (1.0 + gate * (1.0 - sigmoid)))).astype(bf16)
    up_grad = (inner * silu).astype(bf16)

    @pl.when(expert == 0)
    def _():
        slots[...] = jnp.where(lane == expert, slot, 0.0)
        for piece in range(pieces):
            moe_sum[:, piece * wide : (piece + 1) * wide] = nn(scaled, downs[piece, 0])
        back_sum[...] = nt(gate_grad, gate_matrix) + nt(up_grad, up_matrix)

    @pl.when(expert > 0)
    def _():
        slots[...] = jnp.where(lane == expert, slot, slots[...])
        for piece in range(pieces):
            moe_sum[:, piece * wide : (piece + 1) * wide] += nn(scaled, downs[piece, 0])
        back_sum[...] += nt(gate_grad, gate_matrix) + nt(up_grad, up_matrix)

    @pl.when(expert == pl.num_programs(0) - 1)
    def _():
        moe[...] = moe_sum[...].astype(bf16)
        back[...] = back_sum[...].astype(bf16)


def experts_both(rows_in, grads, weight, gates, ups, downs):
    rows, depth = rows_in.shape
    pieces, experts, hidden, wide = downs.shape

    def fixed(shape):
        return pl.BlockSpec(shape, lambda e: (0, 0), pipeline_mode=pl.Buffered(1))

    def of_expert(shape):
        return pl.BlockSpec((shape[0], 1) + shape[2:], lambda e: (0, e, 0, 0))

    return pl.pallas_call(
        experts_kernel,
        grid=(experts,),
        in_specs=[
            fixed((rows, depth)),
            fixed((rows, depth)),
            fixed((rows, experts)),
            of_expert(gates.shape),
            of_expert(ups.shape),
            of_expert(downs.shape),
        ],
        out_specs=[fixed((rows, depth)), fixed((rows, depth)), fixed((rows, experts))],
        out_shape=[
            jax.ShapeDtypeStruct((rows, depth), bf16),
            jax.ShapeDtypeStruct((rows, depth), bf16),
            jax.ShapeDtypeStruct((rows, experts), f32),
        ],
        scratch_shapes=[pltpu.VMEM((rows, depth), f32), pltpu.VMEM((rows, depth), f32)],
        compiler_params=pltpu.CompilerParams(vmem_limit_bytes=60 * MIB),
        cost_estimate=pl.CostEstimate(
            flops=12 * rows * depth * hidden * experts,
            bytes_accessed=6 * depth * hidden * experts,
            transcendentals=rows * hidden * experts,
        ),
    )(rows_in, grads, weight, gates, ups, downs)


def norm_back(values, gain, grad):
    inverse = lax.rsqrt(jnp.mean(values * values, axis=-1, keepdims=True) + EPSILON)
    scaled = values * inverse
    inner = gain * grad
    return inverse * (inner - scaled * jnp.mean(inner * scaled, axis=-1, keepdims=True))


def norm_rows(values, gain):
    inverse = lax.rsqrt(jnp.mean(values * values, axis=-1, keepdims=True) + EPSILON)
    return values * inverse * gain


def per_device(
    n_data,
    n_tensor,
    tokens,
    attn_gain,
    query_gain,
    key_gain,
    query_weight,
    key_weight,
    value_weight,
    output_weight,
    mlp_gain,
    router_weight,
    gate_weight,
    up_weight,
    down_weight,
    query_lower,
    query_raise,
    key_lower,
    key_raise,
    value_lower,
    value_raise,
    output_lower,
    output_raise,
    routes,
    adapter_choice_rows,
    out_cotangent,
):
    local_rows, depth = tokens.shape
    rows = local_rows * n_tensor
    width = query_weight.shape[1]
    adapters, rank = query_raise.shape[:2]
    experts = router_weight.shape[1]
    me = lax.axis_index("tensor")
    first_row = me * local_rows
    adapter = adapter_choice_rows[0]

    def chosen(table):
        return lax.dynamic_index_in_dim(table, adapter, 0, keepdims=False)

    def columns_of(matrix):
        return lax.dynamic_slice_in_dim(matrix, me * width, width, 1)

    tables = rope_tables(rows)
    attn_gain_wide = attn_gain.astype(f32)
    mlp_gain_wide = mlp_gain.astype(f32)
    gains = (query_gain.astype(f32)[None, :], key_gain.astype(f32)[None, :])
    expert_ids = jnp.arange(experts, dtype=jnp.int32)
    route_mask = jnp.any(routes[:, :, None] == expert_ids[None, None, :], axis=1).astype(f32)

    projections = lax.all_gather(
        jnp.concatenate([query_weight, key_weight, value_weight], axis=1),
        "dp",
        axis=0,
        tiled=True,
    )
    output_and_router = lax.all_gather(
        jnp.concatenate([output_weight, router_weight.T], axis=0), "dp", axis=0
    )
    output_full = output_and_router[:, :width].transpose(1, 0, 2).reshape(width, depth)
    router_full = output_and_router[:, width:].transpose(1, 0, 2).reshape(experts, depth)
    gates = lax.all_gather(gate_weight, "dp", axis=0)
    ups = lax.all_gather(up_weight, "dp", axis=0)
    downs = lax.all_gather(down_weight, "dp", axis=0)

    rows_float = tokens.astype(f32)
    normed_local = norm_rows(rows_float, attn_gain_wide).astype(bf16)
    normed = line_gather(normed_local, "tensor", n_tensor)
    cotangent_full = line_gather(after(out_cotangent, normed), "tensor", n_tensor)

    lowers = jnp.concatenate(
        [chosen(query_lower).T, chosen(key_lower).T, chosen(value_lower).T], axis=0
    )
    raises = [chosen(query_raise), chosen(key_raise), chosen(value_raise)]
    mids = nt(normed, lowers).astype(bf16)
    raws = [
        nn(normed, projections[:, i * width : (i + 1) * width])
        + nn(mids[:, i * rank : (i + 1) * rank], raises[i])
        for i in range(3)
    ]
    totals = jnp.stack([jnp.sum(raws[0] * raws[0], axis=1), jnp.sum(raws[1] * raws[1], axis=1)])
    totals = direct_sum(totals, "tensor", n_tensor)
    inverse_rows = lax.rsqrt(totals / depth + EPSILON)
    inverses = (inverse_rows[0][:, None], inverse_rows[1][:, None])
    queries, keys, values, attended, log_sums = attend(raws, inverses, gains, tables)

    output_down = chosen(output_lower).T
    output_up = chosen(output_raise)
    output_mid = nt(attended, output_down)
    attn_part = nn(attended, output_full) + nn(output_mid.astype(bf16), output_up)
    hidden_one = rows_float + line_scatter(attn_part.astype(bf16), "tensor", n_tensor)

    normed_two = line_gather(
        norm_rows(hidden_one, mlp_gain_wide).astype(bf16), "tensor", n_tensor
    )
    route_prob = jax.nn.softmax(nt(normed_two, router_full), axis=-1)
    moe_part, back_part, slot_part = experts_both(
        normed_two, cotangent_full, route_prob * route_mask, gates, ups, downs
    )
    back_local = lax.psum_scatter(back_part, "tensor", scatter_dimension=0, tiled=True)
    prob_grad = direct_scatter((slot_part * route_mask).astype(bf16), "tensor", n_tensor)
    prob_local = lax.dynamic_slice_in_dim(route_prob, first_row, local_rows, 0)
    logit_grad = (
        prob_local * (prob_grad - jnp.sum(prob_local * prob_grad, axis=1, keepdims=True))
    ).astype(bf16)
    normed_two_grad = back_local.astype(f32) + nn(logit_grad, router_full)
    hidden_grad = out_cotangent.astype(f32) + norm_back(
        hidden_one, mlp_gain_wide, normed_two_grad
    )
    attn_grad = lax.all_gather(hidden_grad.astype(bf16), "tensor", axis=0, tiled=True)
    moe_local = lax.psum_scatter(
        after(moe_part, attn_grad), "tensor", scatter_dimension=0, tiled=True
    )
    block_out = (hidden_one + moe_local.astype(f32)).astype(bf16)

    output_mid_grad = nt(attn_grad, output_up).astype(bf16)
    attended_grad = (nt(attn_grad, output_full) + nn(output_mid_grad, output_down)).astype(bf16)
    grad_output_lower = tn(output_mid_grad, attended)
    output_mid_all = direct_sum(output_mid, "tensor", n_tensor).astype(bf16)
    grad_output_raise = tn(output_mid_all, columns_of(attn_grad))

    query_back, key_back, value_raw_grad, query_dot, key_dot = attend_back(
        (queries, keys, values), attended_grad, log_sums, raws, inverses, gains, tables
    )
    dots = direct_sum(jnp.stack([query_dot[:, 0], key_dot[:, 0]]), "tensor", n_tensor) / depth
    raw_grads = [
        (
            inverses[i] * (back - raws[i] * inverses[i] * dots[i][:, None])
        ).astype(bf16)
        for i, back in enumerate((query_back, key_back))
    ] + [value_raw_grad]
    mid_grads = [nt(raw_grads[i], raises[i]) for i in range(3)]
    mid_grads_wide = jnp.concatenate(mid_grads, axis=1)
    normed_part = nn(mid_grads_wide.astype(bf16), lowers)
    for i in range(3):
        normed_part = normed_part + nt(raw_grads[i], projections[:, i * width : (i + 1) * width])
    normed_grad = lax.psum_scatter(
        normed_part.astype(bf16), "tensor", scatter_dimension=0, tiled=True
    )
    input_grad = (
        hidden_grad + norm_back(rows_float, attn_gain_wide, normed_grad.astype(f32))
    ).astype(bf16)

    grad_raises = [tn(mids[:, i * rank : (i + 1) * rank], raw_grads[i]) for i in range(3)]
    mid_grads_all = direct_sum(mid_grads_wide, "tensor", n_tensor).astype(bf16)
    grad_lowers = tn(mid_grads_all, columns_of(normed))
    split = jnp.concatenate(grad_raises + [grad_output_lower], axis=0).astype(bf16)
    full = jnp.concatenate([grad_lowers, grad_output_raise], axis=0).astype(bf16)
    onehot = (adapter == jnp.arange(adapters, dtype=jnp.int32)).astype(f32)
    onehots = lax.all_gather(onehot, "dp", axis=0)
    split_all = lax.all_gather(split, "dp", axis=0)
    full_all = lax.all_gather(full, ("dp", "tensor"), axis=0)

    def by_adapter(pieces):
        return jnp.einsum("ga,grw->arw", onehots, pieces.astype(f32), precision="highest")

    split_sums = [
        by_adapter(split_all[:, i * rank : (i + 1) * rank]) for i in range(4)
    ]
    full_all = full_all.reshape(n_data, n_tensor, 4, rank, width)
    full_sums = [
        by_adapter(full_all[:, :, i].transpose(0, 2, 1, 3).reshape(n_data, rank, depth))
        for i in range(4)
    ]

    def turned(table):
        return table.transpose(0, 2, 1)

    return (
        block_out,
        input_grad,
        turned(full_sums[0]),
        split_sums[0],
        turned(full_sums[1]),
        split_sums[1],
        turned(full_sums[2]),
        split_sums[2],
        turned(split_sums[3]),
        full_sums[3],
    )


def solution(mesh):
    rows = P(("dp", "tensor"), None)
    raised = P(None, None, "tensor")
    in_specs = (
        rows,
        P(),
        P("tensor"),
        P("tensor"),
        P("dp", "tensor"),
        P("dp", "tensor"),
        P("dp", "tensor"),
        P("tensor", "dp"),
        P(),
        P("dp", None),
        P(None, "dp", "tensor"),
        P(None, "dp", "tensor"),
        P(None, "tensor", "dp"),
        P(),
        raised,
        P(),
        raised,
        P(),
        raised,
        P(None, "tensor", None),
        P(),
        P("dp", None),
        P("dp"),
        rows,
    )
    out_specs = (
        rows,
        rows,
        P(),
        raised,
        P(),
        raised,
        P(),
        raised,
        P(None, "tensor", None),
        P(),
    )
    return jax.shard_map(
        functools.partial(per_device, mesh.shape["dp"], mesh.shape["tensor"]),
        mesh=mesh,
        in_specs=in_specs,
        out_specs=out_specs,
        check_vma=False,
    )
```

time: 2050 us -> 1020 us (0.50)
  matrix products: 764 us -> 87.1 us
  waiting for transfers between devices: 1080 us -> 482 us
  Pallas kernels: 0 us -> 158 us
  starting transfers between devices: 1.59 us -> 142 us
  other arithmetic: 81.6 us -> 57.5 us
    dot_general x152 -> x36, matrix products: 764 us -> 87.1 us  [the longest x11 42.9 us: nn(): return jnp.dot(left, right, preferred_element_type=f32)]
    all_gather x11 -> x7, waiting for transfers between devices: 615 us -> 79.6 us  [the longest x1 77.7 us: per_device(): lax.all_gather(hidden_grad.astype(bf16), 'tensor', axis=0, tiled=True)]
    ppermute x0 -> x39, waiting for transfers between devices: none -> 194 us  [the longest x9 124 us: line_gather(): lax.ppermute(lefts[-1], axis, [(i, i - 1) for i in range(1, count - step...]
    pallas_call x0 -> x3, Pallas kernels: none -> 158 us  [the longest x1 125 us: experts_both(): pl.pallas_call(experts_kernel, grid=(experts,), in_specs=[fixed((rows, de...]
    psum x2 -> x0, waiting for transfers between devices: 145 us -> none  [the longest x1 145 us: per_device(): lax.psum((spread(query_down_grad), spread(key_down_grad), spread(value_do...]
    ppermute x0 -> x39, starting transfers between devices: none -> 141 us  [the longest x9 69.8 us: line_gather(): lax.ppermute(rights[-1], axis, [(i, i + 1) for i in range(step - 1, count...]
    reduce_scatter x5 -> x3, waiting for transfers between devices: 311 us -> 206 us  [the longest x1 77.3 us: per_device(): lax.psum_scatter(after(moe_part, attn_grad), 'tensor', scatter_dimension=...]
    convert_element_type x23 -> x11, other arithmetic: 50.8 us -> 19.1 us  [the longest x2 5.86 us: line_scatter(): to_right.astype(bf16)]
  transfers between devices with their start and end apart: 18 -> 49, of which waited for: 15 -> 21; matrix products, arithmetic and copies ran while one was open for 8% -> 16% of each run, Pallas kernels for 0% -> 3%
where the time goes in v1:
time: 1020 us; the launch traced here: 1010 us
  waiting for transfers between devices  482 us (47%)
  Pallas kernels  158 us (15%)
  starting transfers between devices  142 us (14%)
  matrix products  87.1 us (9%)
  other arithmetic  57.5 us (6%)
  local copies, waits for them, and re-layouts  44 us (4%)
  blocking collectives  19.6 us (2%)
  between operations  16.4 us (2%)
    pallas_call x1, Pallas kernels, experts_both(): pl.pallas_call(experts_kernel, grid=(experts,), in_specs=[fixed((rows, de...  125 us
    ppermute x9, waiting for transfers between devices, line_gather(): lax.ppermute(lefts[-1], axis, [(i, i - 1) for i in range(1, count - step...  124 us
    all_gather x1, waiting for transfers between devices, per_device(): lax.all_gather(hidden_grad.astype(bf16), 'tensor', axis=0, tiled=True)  77.7 us
    reduce_scatter x1, waiting for transfers between devices, per_device(): lax.psum_scatter(after(moe_part, attn_grad), 'tensor', scatter_dimension=...  77.3 us
    ppermute x9, starting transfers between devices, line_gather(): lax.ppermute(rights[-1], axis, [(i, i + 1) for i in range(step - 1, count...  69.8 us
    reduce_scatter x1, waiting for transfers between devices, per_device(): lax.psum_scatter(normed_part.astype(bf16), 'tensor', scatter_dimension=0,...  66.2 us
    reduce_scatter x1, waiting for transfers between devices, per_device(): lax.psum_scatter(back_part, 'tensor', scatter_dimension=0, tiled=True)  61.9 us
    dot_general x11, matrix products, nn(): return jnp.dot(left, right, preferred_element_type=f32)  42.9 us
  transfers between devices with their start and end apart: 49, of which 21 were waited for; matrix products, arithmetic and copies ran while one was open for 16% of the time, Pallas kernels for 3%

profile of v1, /device:TPU:0, one launch (start us, length us, event | category | flops | bytes accessed | tf_op | source)
XLA Modules:
  0.0 1005.6 jit_solution(1034733225939856176)
XLA Ops:
  18.9 5.6 collective-permute-start
  24.5 21.4 %collective-permute-done.1 = bf16[256,2048]{1,0:T(8,128)(2,1)S(1)} collective-permute-done((bf16[256,2048]{1,0:T(8,128)(2,1)}, bf16[256,2048]{1,0:T(8,128)(2,1)S(1)}, u32[]{:S(2)}, u32[]{:S(2)}) %collective-permute-start.1) | collective-permute-done | bytes 1048608 | tf_op jit(solution)/shard_map/ppermute | solution.py:45
  48.6 23.6 %collective-permute-done.2 = bf16[256,2048]{1,0:T(8,128)(2,1)} collective-permute-done((bf16[256,2048]{1,0:T(8,128)(2,1)S(1)}, bf16[256,2048]{1,0:T(8,128)(2,1)}, u32[]{:S(2)}, u32[]{:S(2)}) %collective-permute-start.2) | collective-permute-done | bytes 1048608 | tf_op jit(solution)/shard_map/ppermute | solution.py:45
  79.1 18.6 %collective-permute-done.3 = bf16[256,2048]{1,0:T(8,128)(2,1)S(1)} collective-permute-done((bf16[256,2048]{1,0:T(8,128)(2,1)}, bf16[256,2048]{1,0:T(8,128)(2,1)S(1)}, u32[]{:S(2)}, u32[]{:S(2)}) %collective-permute-start.3) | collective-permute-done | bytes 1048608 | tf_op jit(solution)/shard_map/ppermute | solution.py:45
  118.5 6.0 multiply_reduce_fusion.3
  124.6 6.7 multiply_reduce_fusion.2
  134.4 5.9 fusion.29.value_raw
  147.9 15.3 %shard_map.303 = (bf16[1024,512]{1,0:T(8,128)(2,1)S(1)}, bf16[1024,512]{1,0:T(8,128)(2,1)S(1)}, bf16[1024,512]{1,0:T(8,128)(2,1)S(1)}, bf16[1024,512]{1,0:T(8,128)(2,1)S(1)}, f32[4,1024,1]{2,1,0:T(8,128)S(1)}) custom-call(f32[1024,512]{1,0:T(8,128)S(1)} %get-tuple-element.137.query_raw, f32[1024,512]{1,0:T(8,128)S(1)} %copy-done.3, ...), custom_call_target="tpu_custom_call" | custom-call | flops 1073741824 | bytes 10485760 | tf_op jit(solution)/shard_map/pallas_call | solution.py:168
  177.3 17.7 %collective-permute-done.9 = bf16[256,2048]{1,0:T(8,128)(2,1)} collective-permute-done((bf16[256,2048]{1,0:T(8,128)(2,1)S(1)}, bf16[256,2048]{1,0:T(8,128)(2,1)}, u32[]{:S(2)}, u32[]{:S(2)}) %collective-permute-start.9) | collective-permute-done | bytes 1048608 | tf_op jit(solution)/shard_map/ppermute | solution.py:70
  202.4 18.5 %collective-permute-done.10 = bf16[256,2048]{1,0:T(8,128)(2,1)} collective-permute-done((bf16[256,2048]{1,0:T(8,128)(2,1)S(1)}, bf16[256,2048]{1,0:T(8,128)(2,1)}, u32[]{:S(2)}, u32[]{:S(2)}) %collective-permute-start.10) | collective-permute-done | bytes 1048608 | tf_op jit(solution)/shard_map/ppermute | solution.py:70
  227.1 6.2 collective-permute-start.11
  236.3 26.5 %collective-permute-start.21 = (bf16[256,2048]{1,0:T(8,128)(2,1)}, bf16[256,2048]{1,0:T(8,128)(2,1)}, u32[]{:S(2)}, u32[]{:S(2)}) collective-permute-start(bf16[256,2048]{1,0:T(8,128)(2,1)} %param.47), channel_id=1, source_target_pairs={{0,1},{1,2},{2,3},{4,5},{5,6},{6,7},{8,9},{9,10},{10,11},{12,13},{... | collective-permute-start | bytes 3145736 | tf_op jit(solution)/shard_map/ppermute | solution.py:42
  264.1 10.8 %collective-permute-done.14 = bf16[256,2048]{1,0:T(8,128)(2,1)S(1)} collective-permute-done((bf16[256,2048]{1,0:T(8,128)(2,1)S(1)}, bf16[256,2048]{1,0:T(8,128)(2,1)S(1)}, u32[]{:S(2)}, u32[]{:S(2)}) %collective-permute-start.14) | collective-permute-done | bytes 1048608 | tf_op jit(solution)/shard_map/ppermute | solution.py:73
  284.4 11.0 %collective-permute-done.23 = bf16[256,2048]{1,0:T(8,128)(2,1)} collective-permute-done((bf16[256,2048]{1,0:T(8,128)(2,1)S(1)}, bf16[256,2048]{1,0:T(8,128)(2,1)}, u32[]{:S(2)}, u32[]{:S(2)}) %collective-permute-start.23) | collective-permute-done | bytes 1048608 | tf_op jit(solution)/shard_map/ppermute | solution.py:45
  296.7 32.2 %collective-permute-start.15 = (bf16[256,2048]{1,0:T(8,128)(2,1)}, bf16[256,2048]{1,0:T(8,128)(2,1)}, u32[]{:S(2)}, u32[]{:S(2)}) collective-permute-start(bf16[256,2048]{1,0:T(8,128)(2,1)} %get-tuple-element.103), channel_id=1, source_target_pairs={{0,1},{1,2},{2,3},{4,5},{5,6},{6,7},{8,9},{9,10},{10,11},{12,13},{... | collective-permute-start | bytes 3145736 | tf_op jit(solution)/shard_map/ppermute | solution.py:42
  335.2 16.6 %collective-permute-done.24 = bf16[256,2048]{1,0:T(8,128)(2,1)} collective-permute-done((bf16[256,2048]{1,0:T(8,128)(2,1)}, bf16[256,2048]{1,0:T(8,128)(2,1)}, u32[]{:S(2)}, u32[]{:S(2)}) %collective-permute-start.24) | collective-permute-done | bytes 1048608 | tf_op jit(solution)/shard_map/ppermute | solution.py:45
  354.3 15.0 %collective-permute-done.17 = bf16[256,2048]{1,0:T(8,128)(2,1)} collective-permute-done((bf16[256,2048]{1,0:T(8,128)(2,1)}, bf16[256,2048]{1,0:T(8,128)(2,1)}, u32[]{:S(2)}, u32[]{:S(2)}) %collective-permute-start.17) | collective-permute-done | bytes 1048608 | tf_op jit(solution)/shard_map/ppermute | solution.py:45
  373.4 16.6 %collective-permute-done.18 = bf16[256,2048]{1,0:T(8,128)(2,1)S(1)} collective-permute-done((bf16[256,2048]{1,0:T(8,128)(2,1)}, bf16[256,2048]{1,0:T(8,128)(2,1)S(1)}, u32[]{:S(2)}, u32[]{:S(2)}) %collective-permute-start.18) | collective-permute-done | bytes 1048608 | tf_op jit(solution)/shard_map/ppermute | solution.py:45
  404.8 124.6 %shard_map.304 = (bf16[1024,2048]{1,0:T(8,128)(2,1)}, bf16[1024,2048]{1,0:T(8,128)(2,1)}, f32[1024,16]{1,0:T(8,128)}) custom-call(bf16[1024,2048]{1,0:T(8,128)(2,1)} %select_dynamic-update-slice_fusion.3.rows_in, bf16[1024,2048]{1,0:T(8,128)(2,1)} %copy-done.38, f32[1024,16]{1,0:T(8,128)} %get-tuple-element.100.weight, bf16[8,16,256,256]{3,2,1,0:T(8,128)(2,1)} %bitcast.194, ...), custom_call_target="tpu_custom_call" | custom-call | flops 103079215104 | bytes 50331648 | tf_op jit(solution)/shard_map/pallas_call | solution.py:336
  530.6 23.9 %collective-permute-start.29 = (bf16[256,16]{1,0:T(8,128)(2,1)S(1)}, bf16[256,16]{1,0:T(8,128)(2,1)S(1)}, u32[]{:S(2)}, u32[]{:S(2)}) collective-permute-start(bf16[256,16]{1,0:T(8,128)(2,1)S(1)} %get-tuple-element.123), channel_id=1, source_target_pairs={{0,3},{1,0},{2,1},{3,2},{4,7},{5,4},{6,5},{7,6},{8,11},{9,8},{10,9... | collective-permute-start | bytes 24584 | tf_op jit(solution)/shard_map/ppermute | solution.py:88
  557.0 7.3 collective-permute-done.28
  566.4 61.9 %reduce-scatter.4.cloned.1.call-done = bf16[256,2048]{1,0:T(8,128)(2,1)} async-done(((bf16[1024,2048]{1,0:T(8,128)(2,1)}), bf16[256,2048]{1,0:T(8,128)(2,1)}) %reduce-scatter.4.cloned.1.call-update) | async-done | bytes 1048592 | tf_op jit(solution)/shard_map/reduce_scatter | solution.py:474
  637.8 77.7 %all-gather.15.cloned.1.call-done = bf16[1024,2048]{1,0:T(8,128)(2,1)} async-done(((bf16[256,2048]{1,0:T(8,128)(2,1)}), bf16[1024,2048]{1,0:T(8,128)(2,1)}) %all-gather.15.cloned.1.call-update) | async-done | bytes 4194320 | tf_op jit(solution)/shard_map/all_gather | solution.py:484
  723.0 17.9 %shard_map.305 = (f32[1024,512]{1,0:T(8,128)S(1)}, f32[1024,512]{1,0:T(8,128)S(1)}, bf16[1024,512]{1,0:T(8,128)(2,1)S(1)}, f32[1024,1]{1,0:T(8,128)S(1)}, f32[1024,1]{1,0:T(8,128)S(1)}) custom-call(bf16[1024,512]{1,0:T(8,128)(2,1)S(1)} %copy-done.20, bf16[1024,512]{1,0:T(8,128)(2,1)S(1)} %copy-done.22, bf16[1024,512]{1,0:T(8,128)(2,1)S(1)} %copy-done.24, ...), custom_call_target="tpu_custom_call" | custom-call | flops 2684354560 | bytes 14680064 | tf_op jit(solution)/shard_map/pallas_call | solution.py:255
  765.9 11.1 %collective-permute-done.34 = f32[1024,48]{0,1:T(8,128)S(1)} collective-permute-done((f32[1024,48]{0,1:T(8,128)S(1)}, f32[1024,48]{0,1:T(8,128)S(1)}, u32[]{:S(2)}, u32[]{:S(2)}) %collective-permute-start.34) | collective-permute-done | bytes 196640 | tf_op jit(solution)/shard_map/ppermute | solution.py:96
  783.6 7.4 fusion.15
  791.0 7.3 fusion.19
  798.3 9.6 add_convert_fusion
  808.6 8.8 all-gather.4
  818.5 10.7 %all_gather.54 = bf16[8,64,512]{2,1,0:T(8,128)(2,1)S(1)} all-gather(bf16[1,64,512]{2,1,0:T(8,128)(2,1)S(1)} %pad_maximum_fusion.9), channel_id=1, replica_groups=mesh['dp'=8,'tensor'=4] {'dp'}, dimensions={0}, use_global_device_ids=true | all-gather | bytes 589824 | tf_op jit(solution)/shard_map/all_gather | solution.py:525
  847.7 66.2 %reduce-scatter.8.cloned.1.call-done = bf16[256,2048]{1,0:T(8,128)(2,1)} async-done(((bf16[1024,2048]{1,0:T(8,128)(2,1)}), bf16[256,2048]{1,0:T(8,128)(2,1)}) %reduce-scatter.8.cloned.1.call-update) | async-done | bytes 1048592 | tf_op jit(solution)/shard_map/reduce_scatter | solution.py:511
  916.0 77.3 %reduce-scatter.6.cloned.1.call-done = bf16[256,2048]{1,0:T(8,128)(2,1)} async-done(((bf16[1024,2048]{1,0:T(8,128)(2,1)}), bf16[256,2048]{1,0:T(8,128)(2,1)}) %reduce-scatter.6.cloned.1.call-update) | async-done | bytes 1048592 | tf_op jit(solution)/shard_map/reduce_scatter | solution.py:485
  (343 shorter events, 203.3 us)
Async XLA Ops:
  7.2 107.2 %all-gather.19.cloned.1.call-start = ((), (), s32[]{:S(2)}) async-start(), calls=%async_computation.9 | async-start | bytes 2433024 | tf_op jit(solution)/shard_map/all_gather | solution.py:431
  9.0 109.5 %all-gather.13.cloned.1.call-start = ((), (), s32[]{:S(2)}) async-start(), calls=%async_computation.3 | async-start | bytes 7077888 | tf_op jit(solution)/shard_map/all_gather | solution.py:425
  11.1 393.6 %all-gather.21.cloned.1.call-start = ((), (), s32[]{:S(2)}) async-start(), calls=%async_computation.10 | async-start | bytes 18874368 | tf_op jit(solution)/shard_map/all_gather | solution.py:436
  11.9 392.9 %all-gather.23.cloned.1.call-start = ((), (), s32[]{:S(2)}) async-start(), calls=%async_computation.11 | async-start | bytes 18874368 | tf_op jit(solution)/shard_map/all_gather | solution.py:437
  12.5 392.3 %all-gather.25.cloned.1.call-start = ((), (), s32[]{:S(2)}) async-start(), calls=%async_computation.12 | async-start | bytes 18874368 | tf_op jit(solution)/shard_map/all_gather | solution.py:438
  13.0 615.3 %reduce-scatter.4.cloned.1.call-start = ((), (), s32[]{:S(2)}) async-start(), calls=%async_computation.4 | async-start | bytes 5242880 | tf_op jit(solution)/shard_map/reduce_scatter | solution.py:474
  17.6 28.3 %collective-permute-start.1 = (bf16[256,2048]{1,0:T(8,128)(2,1)}, bf16[256,2048]{1,0:T(8,128)(2,1)S(1)}, u32[]{:S(2)}, u32[]{:S(2)}) collective-permute-start(bf16[256,2048]{1,0:T(8,128)(2,1)} %get-tuple-element.107), channel_id=1, source_target_pairs={{1,0},{2,1},{3,2},{5,4},{6,5},{7,6},{9,8},{10,9},{11,10},{13,12},{... | collective-permute-start | bytes 3145736 | tf_op jit(solution)/shard_map/ppermute | solution.py:45
  18.9 29.0 %collective-permute-start = (bf16[256,2048]{1,0:T(8,128)(2,1)}, bf16[256,2048]{1,0:T(8,128)(2,1)S(1)}, u32[]{:S(2)}, u32[]{:S(2)}) collective-permute-start(bf16[256,2048]{1,0:T(8,128)(2,1)} %get-tuple-element.107), channel_id=1, source_target_pairs={{0,1},{1,2},{2,3},{4,5},{5,6},{6,7},{8,9},{9,10},{10,11},{12,13},{... | collective-permute-start | bytes 3145736 | tf_op jit(solution)/shard_map/ppermute | solution.py:42
  45.9 26.3 %collective-permute-start.2 = (bf16[256,2048]{1,0:T(8,128)(2,1)S(1)}, bf16[256,2048]{1,0:T(8,128)(2,1)}, u32[]{:S(2)}, u32[]{:S(2)}) collective-permute-start(bf16[256,2048]{1,0:T(8,128)(2,1)S(1)} %collective-permute-done.1), channel_id=1, source_target_pairs={{1,0},{2,1},{5,4},{6,5},{9,8},{10,9},{13,12},{14,13},{17,16},{18,1... | collective-permute-start | bytes 3145736 | tf_op jit(solution)/shard_map/ppermute | solution.py:45
  47.9 30.4 %collective-permute-start.4 = (bf16[256,2048]{1,0:T(8,128)(2,1)S(1)}, bf16[256,2048]{1,0:T(8,128)(2,1)S(1)}, u32[]{:S(2)}, u32[]{:S(2)}) collective-permute-start(bf16[256,2048]{1,0:T(8,128)(2,1)S(1)} %collective-permute-done), channel_id=1, source_target_pairs={{1,2},{2,3},{5,6},{6,7},{9,10},{10,11},{13,14},{14,15},{17,18},{18... | collective-permute-start | bytes 3145736 | tf_op jit(solution)/shard_map/ppermute | solution.py:42
  72.2 25.5 %collective-permute-start.3 = (bf16[256,2048]{1,0:T(8,128)(2,1)}, bf16[256,2048]{1,0:T(8,128)(2,1)S(1)}, u32[]{:S(2)}, u32[]{:S(2)}) collective-permute-start(bf16[256,2048]{1,0:T(8,128)(2,1)} %collective-permute-done.2), channel_id=1, source_target_pairs={{1,0},{5,4},{9,8},{13,12},{17,16},{21,20},{25,24},{29,28}} | collective-permute-start | bytes 3145736 | tf_op jit(solution)/shard_map/ppermute | solution.py:45
  170.0 24.9 %collective-permute-start.9 = (bf16[256,2048]{1,0:T(8,128)(2,1)S(1)}, bf16[256,2048]{1,0:T(8,128)(2,1)}, u32[]{:S(2)}, u32[]{:S(2)}) collective-permute-start(bf16[256,2048]{1,0:T(8,128)(2,1)S(1)} %get-tuple-element.110), channel_id=1, source_target_pairs={{0,1},{4,5},{8,9},{12,13},{16,17},{20,21},{24,25},{28,29}} | collective-permute-start | bytes 3145736 | tf_op jit(solution)/shard_map/ppermute | solution.py:70
  175.7 26.8 %collective-permute-start.12 = (bf16[256,2048]{1,0:T(8,128)(2,1)S(1)}, bf16[256,2048]{1,0:T(8,128)(2,1)}, u32[]{:S(2)}, u32[]{:S(2)}) collective-permute-start(bf16[256,2048]{1,0:T(8,128)(2,1)S(1)} %get-tuple-element.111), channel_id=1, source_target_pairs={{3,2},{7,6},{11,10},{15,14},{19,18},{23,22},{27,26},{31,30}} | collective-permute-start | bytes 3145736 | tf_op jit(solution)/shard_map/ppermute | solution.py:73
  196.9 24.1 %collective-permute-start.10 = (bf16[256,2048]{1,0:T(8,128)(2,1)S(1)}, bf16[256,2048]{1,0:T(8,128)(2,1)}, u32[]{:S(2)}, u32[]{:S(2)}) collective-permute-start(bf16[256,2048]{1,0:T(8,128)(2,1)S(1)} %add_convert_fusion.7), channel_id=1, source_target_pairs={{0,1},{1,2},{4,5},{5,6},{8,9},{9,10},{12,13},{13,14},{16,17},{17,1... | collective-permute-start | bytes 3145736 | tf_op jit(solution)/shard_map/ppermute | solution.py:70
  225.8 37.0 %collective-permute-start.22 = (bf16[256,2048]{1,0:T(8,128)(2,1)}, bf16[256,2048]{1,0:T(8,128)(2,1)S(1)}, u32[]{:S(2)}, u32[]{:S(2)}) collective-permute-start(bf16[256,2048]{1,0:T(8,128)(2,1)} %param.47), channel_id=1, source_target_pairs={{1,0},{2,1},{3,2},{5,4},{6,5},{7,6},{9,8},{10,9},{11,10},{13,12},{... | collective-permute-start | bytes 3145736 | tf_op jit(solution)/shard_map/ppermute | solution.py:45
  227.1 37.0 %collective-permute-start.11 = (bf16[256,2048]{1,0:T(8,128)(2,1)S(1)}, bf16[256,2048]{1,0:T(8,128)(2,1)S(1)}, u32[]{:S(2)}, u32[]{:S(2)}) collective-permute-start(bf16[256,2048]{1,0:T(8,128)(2,1)S(1)} %get-tuple-element.108), channel_id=1, source_target_pairs={{0,1},{1,2},{2,3},{4,5},{5,6},{6,7},{8,9},{9,10},{10,11},{12,13},{... | collective-permute-start | bytes 3145736 | tf_op jit(solution)/shard_map/ppermute | solution.py:70
  234.9 39.9 %collective-permute-start.14 = (bf16[256,2048]{1,0:T(8,128)(2,1)S(1)}, bf16[256,2048]{1,0:T(8,128)(2,1)S(1)}, u32[]{:S(2)}, u32[]{:S(2)}) collective-permute-start(bf16[256,2048]{1,0:T(8,128)(2,1)S(1)} %add_convert_fusion.4), channel_id=1, source_target_pairs={{3,2},{2,1},{1,0},{7,6},{6,5},{5,4},{11,10},{10,9},{9,8},{15,14},{... | collective-permute-start | bytes 3145736 | tf_op jit(solution)/shard_map/ppermute | solution.py:73
  236.3 46.5 %collective-permute-start.21 = (bf16[256,2048]{1,0:T(8,128)(2,1)}, bf16[256,2048]{1,0:T(8,128)(2,1)}, u32[]{:S(2)}, u32[]{:S(2)}) collective-permute-start(bf16[256,2048]{1,0:T(8,128)(2,1)} %param.47), channel_id=1, source_target_pairs={{0,1},{1,2},{2,3},{4,5},{5,6},{6,7},{8,9},{9,10},{10,11},{12,13},{... | collective-permute-start | bytes 3145736 | tf_op jit(solution)/shard_map/ppermute | solution.py:42
  262.8 32.7 %collective-permute-start.23 = (bf16[256,2048]{1,0:T(8,128)(2,1)S(1)}, bf16[256,2048]{1,0:T(8,128)(2,1)}, u32[]{:S(2)}, u32[]{:S(2)}) collective-permute-start(bf16[256,2048]{1,0:T(8,128)(2,1)S(1)} %collective-permute-done.22), channel_id=1, source_target_pairs={{1,0},{2,1},{5,4},{6,5},{9,8},{10,9},{13,12},{14,13},{17,16},{18,1... | collective-permute-start | bytes 3145736 | tf_op jit(solution)/shard_map/ppermute | solution.py:45
  281.5 48.5 %collective-permute-start.16 = (bf16[256,2048]{1,0:T(8,128)(2,1)}, bf16[256,2048]{1,0:T(8,128)(2,1)}, u32[]{:S(2)}, u32[]{:S(2)}) collective-permute-start(bf16[256,2048]{1,0:T(8,128)(2,1)} %get-tuple-element.103), channel_id=1, source_target_pairs={{1,0},{2,1},{3,2},{5,4},{6,5},{7,6},{9,8},{10,9},{11,10},{13,12},{... | collective-permute-start | bytes 3145736 | tf_op jit(solution)/shard_map/ppermute | solution.py:45
  282.8 51.7 %collective-permute-start.25 = (bf16[256,2048]{1,0:T(8,128)(2,1)}, bf16[256,2048]{1,0:T(8,128)(2,1)}, u32[]{:S(2)}, u32[]{:S(2)}) collective-permute-start(bf16[256,2048]{1,0:T(8,128)(2,1)} %collective-permute-done.21), channel_id=1, source_target_pairs={{1,2},{2,3},{5,6},{6,7},{9,10},{10,11},{13,14},{14,15},{17,18},{18... | collective-permute-start | bytes 3145736 | tf_op jit(solution)/shard_map/ppermute | solution.py:42
  295.4 56.3 %collective-permute-start.24 = (bf16[256,2048]{1,0:T(8,128)(2,1)}, bf16[256,2048]{1,0:T(8,128)(2,1)}, u32[]{:S(2)}, u32[]{:S(2)}) collective-permute-start(bf16[256,2048]{1,0:T(8,128)(2,1)} %collective-permute-done.23), channel_id=1, source_target_pairs={{1,0},{5,4},{9,8},{13,12},{17,16},{21,20},{25,24},{29,28}} | collective-permute-start | bytes 3145736 | tf_op jit(solution)/shard_map/ppermute | solution.py:45
  296.7 56.7 %collective-permute-start.15 = (bf16[256,2048]{1,0:T(8,128)(2,1)}, bf16[256,2048]{1,0:T(8,128)(2,1)}, u32[]{:S(2)}, u32[]{:S(2)}) collective-permute-start(bf16[256,2048]{1,0:T(8,128)(2,1)} %get-tuple-element.103), channel_id=1, source_target_pairs={{0,1},{1,2},{2,3},{4,5},{5,6},{6,7},{8,9},{9,10},{10,11},{12,13},{... | collective-permute-start | bytes 3145736 | tf_op jit(solution)/shard_map/ppermute | solution.py:42
  329.9 39.3 %collective-permute-start.17 = (bf16[256,2048]{1,0:T(8,128)(2,1)}, bf16[256,2048]{1,0:T(8,128)(2,1)}, u32[]{:S(2)}, u32[]{:S(2)}) collective-permute-start(bf16[256,2048]{1,0:T(8,128)(2,1)} %collective-permute-done.16), channel_id=1, source_target_pairs={{1,0},{2,1},{5,4},{6,5},{9,8},{10,9},{13,12},{14,13},{17,16},{18,1... | collective-permute-start | bytes 3145736 | tf_op jit(solution)/shard_map/ppermute | solution.py:45
  334.5 37.7 %collective-permute-start.26 = (bf16[256,2048]{1,0:T(8,128)(2,1)}, bf16[256,2048]{1,0:T(8,128)(2,1)S(1)}, u32[]{:S(2)}, u32[]{:S(2)}) collective-permute-start(bf16[256,2048]{1,0:T(8,128)(2,1)} %collective-permute-done.25), channel_id=1, source_target_pairs={{2,3},{6,7},{10,11},{14,15},{18,19},{22,23},{26,27},{30,31}} | collective-permute-start | bytes 3145736 | tf_op jit(solution)/shard_map/ppermute | solution.py:42
  529.4 186.1 %all-gather.15.cloned.1.call-start = ((), (), s32[]{:S(2)}) async-start(), calls=%async_computation.5 | async-start | bytes 5242880 | tf_op jit(solution)/shard_map/all_gather | solution.py:484
  530.6 26.3 %collective-permute-start.29 = (bf16[256,16]{1,0:T(8,128)(2,1)S(1)}, bf16[256,16]{1,0:T(8,128)(2,1)S(1)}, u32[]{:S(2)}, u32[]{:S(2)}) collective-permute-start(bf16[256,16]{1,0:T(8,128)(2,1)S(1)} %get-tuple-element.123), channel_id=1, source_target_pairs={{0,3},{1,0},{2,1},{3,2},{4,7},{5,4},{6,5},{7,6},{8,11},{9,8},{10,9... | collective-permute-start | bytes 24584 | tf_op jit(solution)/shard_map/ppermute | solution.py:88
  634.8 201.1 %all-gather.17.cloned.1.call-start = ((), (), s32[]{:S(2)}) async-start(), calls=%async_computation.8 | async-start | bytes 2162688 | tf_op jit(solution)/shard_map/all_gather | solution.py:526
  634.9 125.8 %collective-permute-start.38 = (f32[1024,16]{0,1:T(8,128)S(1)}, f32[1024,16]{0,1:T(8,128)S(1)}, u32[]{:S(2)}, u32[]{:S(2)}) collective-permute-start(f32[1024,16]{0,1:T(8,128)S(1)} %copy-done.55), channel_id=1, source_target_pairs={{0,3},{1,0},{2,1},{3,2},{4,7},{5,4},{6,5},{7,6},{8,11},{9,8},{10,9... | collective-permute-start | bytes 196616 | tf_op jit(solution)/shard_map/ppermute | solution.py:96
  637.8 123.5 %collective-permute-start.37 = (f32[1024,16]{0,1:T(8,128)S(1)}, f32[1024,16]{0,1:T(8,128)S(1)}, u32[]{:S(2)}, u32[]{:S(2)}) collective-permute-start(f32[1024,16]{0,1:T(8,128)S(1)} %copy-done.55), channel_id=1, source_target_pairs={{0,2},{1,3},{2,0},{3,1},{4,6},{5,7},{6,4},{7,5},{8,10},{9,11},{10,... | collective-permute-start | bytes 196616 | tf_op jit(solution)/shard_map/ppermute | solution.py:96
  779.2 134.8 %reduce-scatter.8.cloned.1.call-start = ((), (), s32[]{:S(2)}) async-start(), calls=%async_computation.7 | async-start | bytes 5242880 | tf_op jit(solution)/shard_map/reduce_scatter | solution.py:511
  808.0 185.4 %reduce-scatter.6.cloned.1.call-start = ((), (), s32[]{:S(2)}) async-start(), calls=%async_computation.6 | async-start | bytes 5242880 | tf_op jit(solution)/shard_map/reduce_scatter | solution.py:485
  (89 other events, 1719.6 us)
Sparse Core Ops, SparseCore 0:
  10.5 30.8 all-gather.18
  43.9 45.5 all-gather.12
  91.3 89.8 all-gather.20
  183.0 89.8 all-gather.22
  274.6 89.8 all-gather.24
  529.5 98.7 reduce-scatter.3
  635.0 80.4 all-gather.14
  779.3 56.6 all-gather.16
  838.3 75.5 reduce-scatter.7
  916.1 77.2 reduce-scatter.5

commit v2 on v1

v2 whole, which is shorter than its diff:
```python
import functools

import jax
import jax.numpy as jnp
from jax import lax
from jax.experimental import pallas as pl
from jax.experimental.pallas import tpu as pltpu
from jax.sharding import PartitionSpec as P

HEAD_DIM = 128
EPSILON = 1e-05
ROPE_BASE = 10000.0
MASKED = -1e30
MIB = 1024 * 1024
CHUNKS = 2

f32 = jnp.float32
bf16 = jnp.bfloat16


def nn(left, right):
    return jnp.dot(left, right, preferred_element_type=f32)


def nt(left, right):
    return lax.dot_general(left, right, (((1,), (1,)), ((), ())), preferred_element_type=f32)


def tn(left, right):
    return lax.dot_general(left, right, (((0,), (0,)), ((), ())), preferred_element_type=f32)


def after(value, *others):
    return lax.optimization_barrier((value,) + others)[0]


def line_units(unit, axis, count):
    rights, lefts = [unit], [unit]
    for step in range(1, count):
        rights.append(
            lax.ppermute(rights[-1], axis, [(i, i + 1) for i in range(step - 1, count - 1)])
        )
        lefts.append(
            lax.ppermute(lefts[-1], axis, [(i, i - 1) for i in range(1, count - step + 1)])
        )
    return rights[1:], lefts[1:]


def direct_gather(value, axis, count):
    me = lax.axis_index(axis)
    whole = jnp.zeros((count,) + value.shape, value.dtype)
    whole = lax.dynamic_update_index_in_dim(whole, value, me, 0)
    for shift in range(1, count):
        got = lax.ppermute(value, axis, [(i, (i + shift) % count) for i in range(count)])
        whole = lax.dynamic_update_index_in_dim(whole, got, lax.rem(me - shift + count, count), 0)
    return whole


def data_exchanges(count):
    if count == 8:
        first = [i ^ (4 if i & 1 else 2) for i in range(count)]
        second = [i ^ (2 if i & 1 else 4) for i in range(count)]
        return [first, second, [i ^ 1 for i in range(count)]]
    bits = [1 << k for k in range(count.bit_length() - 1)]
    return [[i ^ bit for i in range(count)] for bit in reversed(bits)]


def direct_sum(value, axis, count):
    total = value
    for shift in range(1, count):
        total = total + lax.ppermute(
            value, axis, [(i, (i + shift) % count) for i in range(count)]
        )
    return total


def rope_tables(row_count):
    position = jnp.arange(row_count, dtype=jnp.int32).astype(f32)
    half = HEAD_DIM // 2
    frequency = ROPE_BASE ** (-2.0 * jnp.arange(half, dtype=f32) / HEAD_DIM)
    angles = position[:, None] * frequency[None, :]
    cosine, sine = jnp.cos(angles), jnp.sin(angles)
    return (
        jnp.concatenate([cosine, cosine], axis=1),
        jnp.concatenate([-sine, sine], axis=1),
    )


def as_row(wide):
    return jnp.sum(wide.T, axis=0, keepdims=True)


def as_columns(row):
    return jnp.broadcast_to(row, (128, row.shape[1])).T


def fold_lanes(values):
    total = values[:, :128]
    for first in range(128, values.shape[1], 128):
        total = total + values[:, first : first + 128]
    return total


def project_kernel(count, me, *refs):
    unit = refs[0]
    rights, lefts = refs[1:count], refs[count : 2 * count - 1]
    weights, lowers, query_up, key_up, value_up = refs[2 * count - 1 : 2 * count + 4]
    normed, query_raw, key_raw, values, mids, totals = refs[2 * count + 4 : 2 * count + 10]
    step = pl.program_id(0)
    width = query_up.shape[1]
    rank = query_up.shape[0]

    @pl.when(step == 0)
    def _():
        normed[...] = unit[...]

    for distance in range(1, count):

        @pl.when((step == distance) & (me[0] >= distance))
        def _():
            normed[...] = rights[distance - 1][...]

        @pl.when((step == distance) & (me[0] < distance))
        def _():
            normed[...] = lefts[count - distance - 1][...]

    rows = normed[...]
    mid = nt(rows, lowers[...]).astype(bf16)
    mids[...] = mid

    def raw(place, up):
        return nn(rows, weights[:, place * width : (place + 1) * width]) + nn(
            mid[:, place * rank : (place + 1) * rank], up[...]
        )

    query = raw(0, query_up)
    key = raw(1, key_up)
    query_raw[...] = query
    key_raw[...] = key
    values[...] = raw(2, value_up).astype(bf16)
    totals[0:1, :] = as_row(fold_lanes(query * query))
    totals[1:2, :] = as_row(fold_lanes(key * key))


def project(unit, rights, lefts, weights, lowers, ups, me):
    count = len(rights) + 1
    part, depth = unit.shape
    rows = part * count
    rank, width = ups[0].shape

    def fixed(shape):
        return pl.BlockSpec(shape, lambda s, p: (0, 0), pipeline_mode=pl.Buffered(1))

    def out(columns):
        return pl.BlockSpec((part, columns), lambda s, p: (lax.rem(p[0] - s + count, count), 0))

    return pl.pallas_call(
        functools.partial(project_kernel, count),
        grid_spec=pltpu.PrefetchScalarGridSpec(
            num_scalar_prefetch=1,
            grid=(count,),
            in_specs=[fixed((part, depth))] * (2 * count - 1)
            + [fixed(weights.shape), fixed(lowers.shape)]
            + [fixed((rank, width))] * 3,
            out_specs=[
                out(depth),
                out(width),
                out(width),
                out(width),
                out(3 * rank),
                pl.BlockSpec((2, part), lambda s, p: (0, lax.rem(p[0] - s + count, count))),
            ],
        ),
        out_shape=[
            jax.ShapeDtypeStruct((rows, depth), bf16),
            jax.ShapeDtypeStruct((rows, width), f32),
            jax.ShapeDtypeStruct((rows, width), f32),
            jax.ShapeDtypeStruct((rows, width), bf16),
            jax.ShapeDtypeStruct((rows, 3 * rank), bf16),
            jax.ShapeDtypeStruct((2, rows), f32),
        ],
        compiler_params=pltpu.CompilerParams(vmem_limit_bytes=50 * MIB),
        cost_estimate=pl.CostEstimate(
            flops=6 * rows * depth * width, bytes_accessed=24 * MIB, transcendentals=0
        ),
    )(me[None], unit, *rights, *lefts, weights, lowers, *ups)


def causal_scores(q_block, keys, first):
    scores = nt(q_block, keys) * (HEAD_DIM**-0.5)
    rows = first + lax.broadcasted_iota(jnp.int32, scores.shape, 0)
    columns = lax.broadcasted_iota(jnp.int32, scores.shape, 1)
    return jnp.where(columns <= rows, scores, MASKED)


def attend_kernel(
    block,
    query_raw,
    key_raw,
    values,
    inverses,
    query_gain,
    key_gain,
    cosine,
    sine,
    queries,
    keys,
    attended,
    log_sums,
    wide_inverses,
):
    half = HEAD_DIM // 2
    rows = query_raw.shape[0]

    @pl.when(pl.program_id(0) == 0)
    def _():
        wide_inverses[0] = as_columns(inverses[0:1, :])
        wide_inverses[1] = as_columns(inverses[1:2, :])

    def rotated(raw, place, gain):
        head = raw[...] * wide_inverses[place] * gain[...]
        return (head * cosine[...] + pltpu.roll(head, half, 1) * sine[...]).astype(bf16)

    queries[...] = rotated(query_raw, 0, query_gain)
    keys[...] = rotated(key_raw, 1, key_gain)
    for first in range(0, rows, block):
        end = first + block
        here = slice(first, end)
        scores = causal_scores(queries[here, :], keys[0:end, :], first)
        top = jnp.max(scores, axis=1, keepdims=True)
        exponent = jnp.exp(scores - top)
        total = jnp.sum(exponent, axis=1, keepdims=True)
        soft = (exponent * (1.0 / total)).astype(bf16)
        attended[here, :] = nn(soft, values[0:end, :]).astype(bf16)
        log_sums[0, here, :] = top + jnp.log(total)


def attend(raws, values, inverses, gains, tables):
    rows, width = values.shape
    heads = width // HEAD_DIM
    by_head = pl.BlockSpec((rows, HEAD_DIM), lambda h: (0, h))
    stats = pl.BlockSpec((2, rows), lambda h: (0, 0))
    gain = pl.BlockSpec((1, HEAD_DIM), lambda h: (0, h))
    table = pl.BlockSpec((rows, HEAD_DIM), lambda h: (0, 0))
    wide = jax.ShapeDtypeStruct((rows, width), bf16)
    return pl.pallas_call(
        functools.partial(attend_kernel, min(256, rows)),
        grid=(heads,),
        in_specs=[by_head] * 3 + [stats] + [gain] * 2 + [table] * 2,
        out_specs=[by_head] * 3 + [pl.BlockSpec((1, rows, 1), lambda h: (h, 0, 0))],
        out_shape=[wide] * 3 + [jax.ShapeDtypeStruct((heads, rows, 1), f32)],
        scratch_shapes=[pltpu.VMEM((2, rows, 128), f32)],
        compiler_params=pltpu.CompilerParams(vmem_limit_bytes=40 * MIB),
        cost_estimate=pl.CostEstimate(
            flops=2 * rows * rows * width,
            bytes_accessed=20 * rows * width,
            transcendentals=rows * rows * heads // 2,
        ),
    )(*raws, values, inverses, *gains, *tables)


def attend_back_kernel(
    block,
    queries,
    keys,
    values,
    grads,
    log_sums,
    query_raw,
    key_raw,
    inverses,
    query_gain,
    key_gain,
    cosine,
    sine,
    query_out,
    key_out,
    value_out,
    dots,
    query_grad,
    key_grad,
    value_grad,
    wide_inverses,
    dot_sums,
):
    half = HEAD_DIM // 2
    rows = queries.shape[0]
    scale = HEAD_DIM**-0.5

    @pl.when(pl.program_id(0) == 0)
    def _():
        wide_inverses[0] = as_columns(inverses[0:1, :])
        wide_inverses[1] = as_columns(inverses[1:2, :])
        dot_sums[...] = jnp.zeros_like(dot_sums)

    for first in range(rows - block, -1, -block):
        end = first + block
        here = slice(first, end)
        scores = causal_scores(queries[here, :], keys[0:end, :], first)
        soft = jnp.exp(scores - log_sums[0, here, :])
        soft_grad = nt(grads[here, :], values[0:end, :])
        inner = jnp.sum(soft * soft_grad, axis=1, keepdims=True)
        score_grad = (soft * (soft_grad - inner)).astype(bf16)
        value_part = tn(soft.astype(bf16), grads[here, :])
        key_part = tn(score_grad, queries[here, :])
        query_grad[here, :] = nn(score_grad, keys[0:end, :])
        if end == rows:
            value_grad[...] = value_part
            key_grad[...] = key_part
        else:
            value_grad[0:end, :] += value_part
            key_grad[0:end, :] += key_part

    def pulled(grad, raw, place, gain, out):
        turned = grad[...] * scale
        turned = turned * cosine[...] - pltpu.roll(turned, half, 1) * sine[...]
        turned = turned * gain[...]
        out[...] = turned
        dot_sums[place] += turned * (raw[...] * wide_inverses[place])

    pulled(query_grad, query_raw, 0, query_gain, query_out)
    pulled(key_grad, key_raw, 1, key_gain, key_out)
    value_out[...] = value_grad[...].astype(bf16)

    @pl.when(pl.program_id(0) == pl.num_programs(0) - 1)
    def _():
        dots[0:1, :] = as_row(dot_sums[0])
        dots[1:2, :] = as_row(dot_sums[1])


def attend_back(heads_in, grads, log_sums, raws, inverses, gains, tables):
    rows, width = grads.shape
    heads = width // HEAD_DIM
    by_head = pl.BlockSpec((rows, HEAD_DIM), lambda h: (0, h))
    stats = pl.BlockSpec((2, rows), lambda h: (0, 0))
    gain = pl.BlockSpec((1, HEAD_DIM), lambda h: (0, h))
    table = pl.BlockSpec((rows, HEAD_DIM), lambda h: (0, 0))
    return pl.pallas_call(
        functools.partial(attend_back_kernel, min(256, rows)),
        grid=(heads,),
        in_specs=[by_head] * 4
        + [pl.BlockSpec((1, rows, 1), lambda h: (h, 0, 0))]
        + [by_head] * 2
        + [stats]
        + [gain] * 2
        + [table] * 2,
        out_specs=[by_head] * 3 + [stats],
        out_shape=[
            jax.ShapeDtypeStruct((rows, width), f32),
            jax.ShapeDtypeStruct((rows, width), f32),
            jax.ShapeDtypeStruct((rows, width), bf16),
            jax.ShapeDtypeStruct((2, rows), f32),
        ],
        scratch_shapes=[pltpu.VMEM((rows, HEAD_DIM), f32)] * 3
        + [pltpu.VMEM((2, rows, 128), f32)] * 2,
        compiler_params=pltpu.CompilerParams(vmem_limit_bytes=50 * MIB),
        cost_estimate=pl.CostEstimate(
            flops=5 * rows * rows * width,
            bytes_accessed=28 * rows * width,
            transcendentals=rows * rows * heads // 2,
        ),
    )(*heads_in, grads, log_sums, *raws, inverses, *gains, *tables)


def project_back_kernel(
    query_back,
    key_back,
    value_grads,
    query_raw,
    key_raw,
    inverses,
    dots,
    weights,
    lowers,
    query_up,
    key_up,
    value_up,
    part,
    raw_grads,
    mid_grads,
):
    width = query_back.shape[1]
    rank = query_up.shape[0]

    def raw_grad(back, raw, place):
        inverse = as_columns(inverses[place : place + 1, :])
        dot = as_columns(dots[place : place + 1, :]) * inverse
        for first in range(0, width, 128):
            here = slice(first, first + 128)
            grad = inverse * (back[:, here] - raw[:, here] * dot)
            raw_grads[:, place * width + first : place * width + first + 128] = grad.astype(bf16)

    raw_grad(query_back, query_raw, 0)
    raw_grad(key_back, key_raw, 1)
    raw_grads[:, 2 * width :] = value_grads[...]
    total = nt(raw_grads[...], weights[...])
    for place, up in enumerate((query_up, key_up, value_up)):
        here = slice(place * rank, (place + 1) * rank)
        mid = nt(raw_grads[:, place * width : (place + 1) * width], up[...])
        mid_grads[:, here] = mid
        total += nn(mid.astype(bf16), lowers[here, :])
    part[...] = total.astype(bf16)


def project_back(backs, value_grads, raws, inverses, dots, weights, lowers, ups):
    rows, width = value_grads.shape
    rank = ups[0].shape[0]
    depth = weights.shape[0]
    block = min(256, rows)

    def fixed(shape):
        return pl.BlockSpec(shape, lambda s: (0, 0), pipeline_mode=pl.Buffered(1))

    def rowwise(columns):
        return pl.BlockSpec((block, columns), lambda s: (s, 0))

    stats = pl.BlockSpec((2, block), lambda s: (0, s))
    return pl.pallas_call(
        project_back_kernel,
        grid=(rows // block,),
        in_specs=[rowwise(width)] * 5
        + [stats] * 2
        + [fixed(weights.shape), fixed(lowers.shape)]
        + [fixed((rank, width))] * 3,
        out_specs=[rowwise(depth), rowwise(3 * width), rowwise(3 * rank)],
        out_shape=[
            jax.ShapeDtypeStruct((rows, depth), bf16),
            jax.ShapeDtypeStruct((rows, 3 * width), bf16),
            jax.ShapeDtypeStruct((rows, 3 * rank), f32),
        ],
        compiler_params=pltpu.CompilerParams(vmem_limit_bytes=50 * MIB),
        cost_estimate=pl.CostEstimate(
            flops=6 * rows * depth * width, bytes_accessed=24 * MIB, transcendentals=0
        ),
    )(*backs, value_grads, *raws, inverses, dots, weights, lowers, *ups)


def experts_kernel(pieces, group, splits, sources, rows_in, grads, weight, *refs):
    shards = refs[:pieces]
    moe, back, gates, ups, downs, moe_sum, back_sum, slots, arrived = refs[-9:]
    step = pl.program_id(0)
    steps = pl.num_programs(0)
    rows, experts = weight.shape
    depth = moe_sum.shape[1]
    wide = depth // pieces
    hidden = gates.shape[-1]

    def copies(at_step, slot):
        made = []
        for index in range(pieces):
            place = pl.ds(pl.multiple_of(sources[index] * wide, wide), wide)
            for member in range(group):
                expert = at_step * group + member
                targets = (
                    gates.at[slot, member, place],
                    ups.at[slot, member, place],
                    downs.at[slot, pl.ds(member * hidden, hidden), place],
                )
                for kind, target in enumerate(targets):
                    made.append(
                        pltpu.make_async_copy(
                            shards[index].at[kind * experts + expert],
                            target,
                            arrived.at[slot, kind, member, index],
                        )
                    )
        return made

    @pl.when(step == 0)
    def _():
        for copy in copies(0, 0):
            copy.start()
        slots[...] = jnp.zeros_like(slots)
        moe_sum[...] = jnp.zeros_like(moe_sum)
        back_sum[...] = jnp.zeros_like(back_sum)

    slot = lax.rem(step, 2)

    @pl.when(step + 1 < steps)
    def _():
        for copy in copies(step + 1, 1 - slot):
            copy.start()

    for copy in copies(step, slot):
        copy.wait()

    grads_all = grads[...].reshape(rows, depth)
    down = downs[slot]
    part = rows // splits
    for split in range(splits):
        here = slice(split * part, (split + 1) * part)
        row_block = rows_in[here, :]
        weight_block = weight[here, :]
        lane = lax.broadcasted_iota(jnp.int32, weight_block.shape, 1)
        inner_all = nt(grads_all[here, :], down)
        scaled_all = []
        back_block = None
        slot_block = None
        for member in range(group):
            expert = step * group + member
            gate = nn(row_block, gates[slot, member])
            up = nn(row_block, ups[slot, member])
            inner = inner_all[:, member * hidden : (member + 1) * hidden]
            row_scale = jnp.sum(
                jnp.where(lane == expert, weight_block, 0.0), axis=1, keepdims=True
            )
            sigmoid = jax.nn.sigmoid(gate)
            silu = gate * sigmoid
            activated = (silu * up).astype(bf16).astype(f32)
            slot_grad = jnp.where(
                lane == expert, jnp.sum(activated * inner, axis=1, keepdims=True), 0.0
            )
            scaled_all.append((row_scale * activated).astype(bf16))
            inner = row_scale * inner
            gate_grad = (inner * up * (sigmoid * (1.0 + gate * (1.0 - sigmoid)))).astype(bf16)
            up_grad = (inner * silu).astype(bf16)
            back_part = nt(gate_grad, gates[slot, member]) + nt(up_grad, ups[slot, member])
            back_block = back_part if back_block is None else back_block + back_part
            slot_block = slot_grad if slot_block is None else slot_block + slot_grad
        scaled = scaled_all[0] if group == 1 else jnp.concatenate(scaled_all, axis=1)
        slots[here, :] += slot_block
        moe_sum[here, :] += nn(scaled, down)
        back_sum[here, :] += back_block

    @pl.when(step == steps - 1)
    def _():
        moe[...] = moe_sum[...].astype(bf16).reshape(moe.shape)
        back[:, :depth] = back_sum[...].astype(bf16)
        back[:, depth:] = jnp.zeros((rows, back.shape[1] - depth), bf16)
        back[:, depth : depth + experts] = slots[...].astype(bf16)


def experts_both(rows_in, grads, weight, shards, sources, chunk, earlier):
    rows, depth = rows_in.shape
    units, _, part, _ = grads.shape
    experts = weight.shape[1]
    pieces = len(shards)
    hidden = shards[0].shape[2]
    group = 2

    def fixed(shape):
        return pl.BlockSpec(shape, lambda e, s: (0, 0), pipeline_mode=pl.Buffered(1))

    of_chunk = pl.BlockSpec(
        (units, 1, part, depth), lambda e, s: (0, chunk, 0, 0), pipeline_mode=pl.Buffered(1)
    )
    anywhere = pl.BlockSpec(memory_space=pl.ANY)
    in_specs = [fixed((rows, depth)), of_chunk, fixed((rows, experts))] + [anywhere] * pieces
    operands = [rows_in, grads, weight, *shards]
    aliases = {}
    if earlier is not None:
        in_specs.append(anywhere)
        operands.append(earlier)
        aliases = {len(operands): 0}
    return pl.pallas_call(
        functools.partial(experts_kernel, pieces, group, 2),
        grid_spec=pltpu.PrefetchScalarGridSpec(
            num_scalar_prefetch=1,
            grid=(experts // group,),
            in_specs=in_specs,
            out_specs=[of_chunk, fixed((rows, depth + 128))],
            scratch_shapes=[
                pltpu.VMEM((2, group, depth, hidden), bf16),
                pltpu.VMEM((2, group, depth, hidden), bf16),
                pltpu.VMEM((2, group * hidden, depth), bf16),
                pltpu.VMEM((rows, depth), f32),
                pltpu.VMEM((rows, depth), f32),
                pltpu.VMEM((rows, experts), f32),
                pltpu.SemaphoreType.DMA((2, 3, group, pieces)),
            ],
        ),
        out_shape=[
            jax.ShapeDtypeStruct(grads.shape, bf16),
            jax.ShapeDtypeStruct((rows, depth + 128), bf16),
        ],
        input_output_aliases=aliases,
        compiler_params=pltpu.CompilerParams(vmem_limit_bytes=58 * MIB),
        cost_estimate=pl.CostEstimate(
            flops=12 * rows * depth * hidden * experts,
            bytes_accessed=6 * depth * hidden * experts,
            transcendentals=rows * hidden * experts,
        ),
    )(sources, *operands)


def norm_back(values, gain, grad):
    inverse = lax.rsqrt(jnp.mean(values * values, axis=-1, keepdims=True) + EPSILON)
    scaled = values * inverse
    inner = gain * grad
    return inverse * (inner - scaled * jnp.mean(inner * scaled, axis=-1, keepdims=True))


def norm_rows(values, gain):
    inverse = lax.rsqrt(jnp.mean(values * values, axis=-1, keepdims=True) + EPSILON)
    return values * inverse * gain


def per_device(
    n_data,
    n_tensor,
    tokens,
    attn_gain,
    query_gain,
    key_gain,
    query_weight,
    key_weight,
    value_weight,
    output_weight,
    mlp_gain,
    router_weight,
    gate_weight,
    up_weight,
    down_weight,
    query_lower,
    query_raise,
    key_lower,
    key_raise,
    value_lower,
    value_raise,
    output_lower,
    output_raise,
    routes,
    adapter_choice_rows,
    out_cotangent,
):
    local_rows, depth = tokens.shape
    rows = local_rows * n_tensor
    width = query_weight.shape[1]
    adapters, rank = query_raise.shape[:2]
    experts = router_weight.shape[1]
    me = lax.axis_index("tensor")
    first_row = me * local_rows
    adapter = adapter_choice_rows[0]

    def chosen(table):
        return lax.dynamic_index_in_dim(table, adapter, 0, keepdims=False)

    def columns_of(matrix):
        return lax.dynamic_slice_in_dim(matrix, me * width, width, 1)

    attn_gain_wide = attn_gain.astype(f32)
    mlp_gain_wide = mlp_gain.astype(f32)
    gains = (query_gain.astype(f32)[None, :], key_gain.astype(f32)[None, :])
    expert_ids = jnp.arange(experts, dtype=jnp.int32)

    projections = lax.all_gather(
        jnp.concatenate([query_weight, key_weight, value_weight], axis=1),
        "dp",
        axis=0,
        tiled=True,
    )
    output_and_router = lax.all_gather(
        jnp.concatenate([output_weight, router_weight.T], axis=0), "dp", axis=0
    )
    output_full = output_and_router[:, :width].transpose(1, 0, 2).reshape(width, depth)
    router_full = output_and_router[:, width:].transpose(1, 0, 2).reshape(experts, depth)

    rows_float = tokens.astype(f32)
    normed_local = norm_rows(rows_float, attn_gain_wide).astype(bf16)

    exchanges = data_exchanges(n_data)

    def swap(value, partners):
        return lax.ppermute(value, "dp", list(enumerate(partners)))

    sources = [list(range(n_data))]
    for partners in exchanges:
        sources += [[known[partner] for partner in partners] for known in sources]
    my_sources = jnp.array(sources, jnp.int32).T[lax.axis_index("dp")]
    shard = jnp.concatenate(
        [after(gate_weight, normed_local), up_weight, down_weight], axis=0
    )
    shards = [shard]

    rights, lefts = line_units(normed_local, "tensor", n_tensor)
    cotangent_full = lax.all_gather(out_cotangent, "tensor", axis=0, tiled=True)
    tables = rope_tables(rows)
    lowers = jnp.concatenate(
        [chosen(query_lower).T, chosen(key_lower).T, chosen(value_lower).T], axis=0
    )
    raises = [chosen(query_raise), chosen(key_raise), chosen(value_raise)]
    normed, query_raw, key_raw, values, mids, totals = project(
        normed_local, rights, lefts, projections, lowers, raises, me
    )
    raws = (query_raw, key_raw)
    inverses = lax.rsqrt(direct_sum(totals, "tensor", n_tensor) / depth + EPSILON)
    queries, keys, attended, log_sums = attend(raws, values, inverses, gains, tables)

    for number, partners in enumerate(exchanges):
        held = []
        for index, piece in enumerate(shards):
            if index == 0:
                held.append(swap(piece, partners))
            elif number < len(exchanges) - 1 or index < len(shards) - 1:
                held.append(swap(after(piece, attended), partners))
            else:
                held.append(None)
        shards += held

    output_down = chosen(output_lower).T
    output_up = chosen(output_raise)
    output_mid = nt(attended, output_down)
    attn_part = nn(attended, output_full) + nn(output_mid.astype(bf16), output_up)
    hidden_one = rows_float + lax.psum_scatter(
        attn_part.astype(bf16), "tensor", scatter_dimension=0, tiled=True
    ).astype(f32)
    normed_two = norm_rows(hidden_one, mlp_gain_wide).astype(bf16)
    last = len(shards) // 2 - 1
    shards[-1] = swap(after(shards[last], normed_two), exchanges[-1])

    prob_local = jax.nn.softmax(nt(normed_two, router_full), axis=-1)
    part = local_rows // CHUNKS
    grads_view = cotangent_full.reshape(n_tensor, CHUNKS, part, depth)
    routes_view = routes.reshape(n_tensor, CHUNKS, part, routes.shape[1])
    moe_part = None
    back_parts = []
    for chunk in range(CHUNKS):
        chunk_rows = lax.all_gather(
            normed_two[chunk * part : (chunk + 1) * part], "tensor", axis=0, tiled=True
        )
        chunk_routes = routes_view[:, chunk].reshape(n_tensor * part, routes.shape[1])
        chosen_experts = jnp.any(chunk_routes[:, :, None] == expert_ids[None, None, :], axis=1)
        probability = jax.nn.softmax(nt(chunk_rows, router_full), axis=-1)
        moe_part, back_part = experts_both(
            chunk_rows,
            grads_view,
            jnp.where(chosen_experts, probability, 0.0),
            shards,
            my_sources,
            chunk,
            moe_part,
        )
        back_parts.append(
            lax.psum_scatter(back_part, "tensor", scatter_dimension=0, tiled=True)
        )
    back_local = jnp.concatenate(back_parts, axis=0).astype(f32)
    local_routes = lax.dynamic_slice_in_dim(routes, first_row, local_rows, 0)
    local_mask = jnp.any(local_routes[:, :, None] == expert_ids[None, None, :], axis=1)
    prob_grad = jnp.where(local_mask, back_local[:, depth : depth + experts], 0.0)
    logit_grad = (
        prob_local * (prob_grad - jnp.sum(prob_local * prob_grad, axis=1, keepdims=True))
    ).astype(bf16)
    normed_two_grad = back_local[:, :depth] + nn(logit_grad, router_full)
    hidden_grad = out_cotangent.astype(f32) + norm_back(
        hidden_one, mlp_gain_wide, normed_two_grad
    )
    attn_grad = lax.all_gather(hidden_grad.astype(bf16), "tensor", axis=0, tiled=True)
    moe_local = lax.psum_scatter(
        after(moe_part.reshape(rows, depth), attn_grad), "tensor", scatter_dimension=0, tiled=True
    )
    block_out = (hidden_one + moe_local.astype(f32)).astype(bf16)

    output_mid_grad = nt(attn_grad, output_up).astype(bf16)
    attended_grad = (nt(attn_grad, output_full) + nn(output_mid_grad, output_down)).astype(bf16)
    query_back, key_back, value_grads, dots = attend_back(
        (queries, keys, values), attended_grad, log_sums, raws, inverses, gains, tables
    )
    dots = direct_sum(dots, "tensor", n_tensor) / depth
    normed_part, raw_grads, mid_grads = project_back(
        (query_back, key_back), value_grads, raws, inverses, dots, projections, lowers, raises
    )
    normed_grad = lax.psum_scatter(normed_part, "tensor", scatter_dimension=0, tiled=True)
    input_grad = (
        hidden_grad + norm_back(rows_float, attn_gain_wide, normed_grad.astype(f32))
    ).astype(bf16)

    grad_output_lower = tn(output_mid_grad, attended)
    sums = direct_sum(jnp.concatenate([mid_grads, output_mid], axis=1), "tensor", n_tensor)
    grad_lowers = tn(sums[:, : 3 * rank].astype(bf16), columns_of(normed))
    grad_output_raise = tn(sums[:, 3 * rank :].astype(bf16), columns_of(attn_grad))
    grad_raises = tn(mids, raw_grads)
    grad_raises = [
        grad_raises[i * rank : (i + 1) * rank, i * width : (i + 1) * width] for i in range(3)
    ]
    full = jnp.concatenate([grad_lowers, grad_output_raise], axis=0).astype(bf16)
    full = direct_gather(full, "tensor", n_tensor).reshape(n_tensor * 4 * rank, width)
    onehot = jnp.broadcast_to(
        (adapter == jnp.arange(adapters, dtype=jnp.int32)).astype(bf16)[:, None],
        (adapters, width),
    )
    onehot = jnp.concatenate([onehot, jnp.zeros((16 - adapters, width), bf16)], axis=0)
    split = jnp.concatenate(grad_raises + [grad_output_lower], axis=0).astype(bf16)
    gathered = jnp.concatenate([full, split, onehot], axis=0)[None]
    for partners in reversed(data_exchanges(n_data)[:-1]):
        gathered = jnp.concatenate([gathered, swap(gathered, partners)], axis=0)
    gathered = jnp.concatenate([gathered, swap(gathered, exchanges[-1])], axis=0)
    onehots = gathered[:, -16 : adapters - 16, 0]
    by_adapter = jnp.einsum(
        "ga,grw->arw", onehots, gathered[:, :-16], preferred_element_type=f32
    )
    split_sums = [
        by_adapter[:, (4 * n_tensor + i) * rank : (4 * n_tensor + i + 1) * rank]
        for i in range(4)
    ]
    full_sums = by_adapter[:, : 4 * n_tensor * rank].reshape(
        adapters, n_tensor, 4, rank, width
    )
    full_sums = [
        full_sums[:, :, i].transpose(0, 2, 1, 3).reshape(adapters, rank, depth) for i in range(4)
    ]

    def turned(table):
        return table.transpose(0, 2, 1)

    return (
        block_out,
        input_grad,
        turned(full_sums[0]),
        split_sums[0],
        turned(full_sums[1]),
        split_sums[1],
        turned(full_sums[2]),
        split_sums[2],
        turned(split_sums[3]),
        full_sums[3],
    )


def solution(mesh):
    rows = P(("dp", "tensor"), None)
    raised = P(None, None, "tensor")
    in_specs = (
        rows,
        P(),
        P("tensor"),
        P("tensor"),
        P("dp", "tensor"),
        P("dp", "tensor"),
        P("dp", "tensor"),
        P("tensor", "dp"),
        P(),
        P("dp", None),
        P(None, "dp", "tensor"),
        P(None, "dp", "tensor"),
        P(None, "tensor", "dp"),
        P(),
        raised,
        P(),
        raised,
        P(),
        raised,
        P(None, "tensor", None),
        P(),
        P("dp", None),
        P("dp"),
        rows,
    )
    out_specs = (
        rows,
        rows,
        P(),
        raised,
        P(),
        raised,
        P(),
        raised,
        P(None, "tensor", None),
        P(),
    )
    return jax.shard_map(
        functools.partial(per_device, mesh.shape["dp"], mesh.shape["tensor"]),
        mesh=mesh,
        in_specs=in_specs,
        out_specs=out_specs,
        check_vma=False,
    )
```

time: 1020 us -> 992 us (0.973)
  waiting for transfers between devices: 482 us -> 597 us
  starting transfers between devices: 142 us -> 35.6 us
  matrix products: 87.1 us -> 37.4 us
  Pallas kernels: 158 us -> 202 us
  other arithmetic: 57.5 us -> 33.1 us
  local copies, waits for them, and re-layouts: 44 us -> 64 us
  blocking collectives: 19.6 us -> 0 us
    ppermute x27 -> x19, starting transfers between devices: 128 us -> 26.8 us  [the longest x3 8.67 us: direct_gather(): lax.ppermute(value, axis, [(i, (i + shift) % count) for i in range(count)])]
    ppermute x12 -> x9, waiting for transfers between devices: 15 us -> 93.3 us  [direct_sum(): lax.ppermute(value, axis, [(i, (i + shift) % count) for i in range(count)])]
    pallas_call x1 -> x4, Pallas kernels: 125 us -> 174 us  [the longest x2 139 us: experts_both(): pl.pallas_call(functools.partial(experts_kernel, pieces, group, 2), grid_...]
    reduce_scatter x2 -> x3, waiting for transfers between devices: 144 us -> 99.1 us  [the longest x1 68.3 us: per_device(): lax.psum_scatter(attn_part.astype(bf16), 'tensor', scatter_dimension=0, t...]
    ppermute x27 -> x19, waiting for transfers between devices: 179 us -> 222 us  [the longest x10 154 us: swap(): return lax.ppermute(value, 'dp', list(enumerate(partners)))]
    dot_general x11 -> x4, matrix products: 42.9 us -> 10 us  [nn(): return jnp.dot(left, right, preferred_element_type=f32)]
    reduce_scatter x1 -> x2, waiting for transfers between devices: 61.9 us -> 84.9 us  [per_device(): lax.psum_scatter(back_part, 'tensor', scatter_dimension=0, tiled=True)]
    dot_general x11 -> x6, matrix products: 36.5 us -> 16.2 us  [nt(): lax.dot_general(left, right, (((1,), (1,)), ((), ())), preferred_element_...]
  transfers between devices with their start and end apart: 49 -> 39, of which waited for: 21 -> 21; matrix products, arithmetic and copies ran while one was open for 16% -> 9% of each run, Pallas kernels for 3% -> 2%
where the time goes in v2:
time: 992 us; the launch traced here: 985 us
  waiting for transfers between devices  597 us (60%)
  Pallas kernels  202 us (20%)
  local copies, waits for them, and re-layouts  64 us (6%)
  matrix products  37.4 us (4%)
  starting transfers between devices  35.6 us (4%)
  other arithmetic  33.1 us (3%)
  between operations  15.8 us (2%)
    ppermute x10, waiting for transfers between devices, swap(): return lax.ppermute(value, 'dp', list(enumerate(partners)))  154 us
    pallas_call x2, Pallas kernels, experts_both(): pl.pallas_call(functools.partial(experts_kernel, pieces, group, 2), grid_...  139 us
    ppermute x9, waiting for transfers between devices, direct_sum(): lax.ppermute(value, axis, [(i, (i + shift) % count) for i in range(count)])  93.3 us
    reduce_scatter x2, waiting for transfers between devices, per_device(): lax.psum_scatter(back_part, 'tensor', scatter_dimension=0, tiled=True)  84.9 us
    all_gather x1, waiting for transfers between devices, per_device(): lax.all_gather(hidden_grad.astype(bf16), 'tensor', axis=0, tiled=True)  80.1 us
    reduce_scatter x1, waiting for transfers between devices, per_device(): lax.psum_scatter(attn_part.astype(bf16), 'tensor', scatter_dimension=0, t...  68.3 us
    ppermute x3, waiting for transfers between devices, line_units(): lax.ppermute(lefts[-1], axis, [(i, i - 1) for i in range(1, count - step...  43.8 us
    reduce_scatter x1, waiting for transfers between devices, per_device(): lax.psum_scatter(after(moe_part.reshape(rows, depth), attn_grad), 'tensor...  30.9 us
  transfers between devices with their start and end apart: 39, of which 21 were waited for; matrix products, arithmetic and copies ran while one was open for 9% of the time, Pallas kernels for 2%

profile of v2, /device:TPU:0, one launch (start us, length us, event | category | flops | bytes accessed | tf_op | source)
XLA Modules:
  0.0 984.6 jit_solution(6938029898796317925)
XLA Ops:
  10.2 5.0 collective-permute-start
  17.3 20.2 %collective-permute-done.refs_1_ = bf16[256,2048]{1,0:T(8,128)(2,1)S(1)} collective-permute-done((bf16[256,2048]{1,0:T(8,128)(2,1)S(1)}, bf16[256,2048]{1,0:T(8,128)(2,1)S(1)}, u32[]{:S(2)}, u32[]{:S(2)}) %collective-permute-start) | collective-permute-done | bytes 1048608 | tf_op jit(solution)/shard_map/ppermute | solution.py:41
  47.0 21.8 %collective-permute-done.4.refs_5_ = bf16[256,2048]{1,0:T(8,128)(2,1)} collective-permute-done((bf16[256,2048]{1,0:T(8,128)(2,1)}, bf16[256,2048]{1,0:T(8,128)(2,1)}, u32[]{:S(2)}, u32[]{:S(2)}) %collective-permute-start.4) | collective-permute-done | bytes 1048608 | tf_op jit(solution)/shard_map/ppermute | solution.py:44
  74.9 19.3 %collective-permute-done.5.refs_6_ = bf16[256,2048]{1,0:T(8,128)(2,1)} collective-permute-done((bf16[256,2048]{1,0:T(8,128)(2,1)}, bf16[256,2048]{1,0:T(8,128)(2,1)}, u32[]{:S(2)}, u32[]{:S(2)}) %collective-permute-start.5) | collective-permute-done | bytes 1048608 | tf_op jit(solution)/shard_map/ppermute | solution.py:44
  95.4 17.7 %shard_map.312 = (bf16[1024,2048]{1,0:T(8,128)(2,1)}, f32[1024,512]{1,0:T(8,128)}, f32[1024,512]{1,0:T(8,128)}, bf16[1024,512]{1,0:T(8,128)(2,1)S(1)}, bf16[1024...) custom-call(s32[1]{0:T(128)} %bitcast.me, bf16[256,2048]{1,0:T(8,128)(2,1)S(1)} %fusion.6.refs_0_, ...), custom_call_target="tpu_custom_call" | custom-call | flops 6442450944 | bytes 25165824 | tf_op jit(solution)/shard_map/pallas_call | solution.py:157
  119.5 4.1 copy.146
  127.5 11.2 %shard_map.313 = (bf16[1024,512]{1,0:T(8,128)(2,1)S(1)}, bf16[1024,512]{1,0:T(8,128)(2,1)S(1)}, bf16[1024,512]{1,0:T(8,128)(2,1)S(1)}, f32[4,1024,1]{2,1,0:T(8,128)S(1)}) custom-call(f32[1024,512]{1,0:T(8,128)S(1)} %copy-done.1, f32[1024,512]{1,0:T(8,128)S(1)} %copy-done.2, bf16[1024,512]{1,0:T(8,128)(2,1)S(1)} %copy-done.8, ...), custom_call_target="tpu_custom_call" | custom-call | flops 1073741824 | bytes 10485760 | tf_op jit(solution)/shard_map/pallas_call | solution.py:246
  142.1 4.3 add_convert_fusion
  155.7 68.3 %reduce-scatter.6.cloned.1.call-done = bf16[256,2048]{1,0:T(8,128)(2,1)} async-done(((bf16[1024,2048]{1,0:T(8,128)(2,1)}), bf16[256,2048]{1,0:T(8,128)(2,1)}) %reduce-scatter.6.cloned.1.call-update) | async-done | bytes 1048592 | tf_op jit(solution)/shard_map/reduce_scatter | solution.py:704
  231.4 68.2 %collective-permute-done.10.refs_2_ = bf16[48,256,256]{2,1,0:T(8,128)(2,1)} collective-permute-done((bf16[48,256,256]{2,1,0:T(8,128)(2,1)}, bf16[48,256,256]{2,1,0:T(8,128)(2,1)}, u32[]{:S(2)}, u32[]{:S(2)}) %collective-permute-start.10) | collective-permute-done | bytes 6291488 | tf_op jit(solution)/shard_map/ppermute | solution.py:664
  299.6 67.4 %collective-permute-done.11.refs_3_ = bf16[48,256,256]{2,1,0:T(8,128)(2,1)} collective-permute-done((bf16[48,256,256]{2,1,0:T(8,128)(2,1)}, bf16[48,256,256]{2,1,0:T(8,128)(2,1)}, u32[]{:S(2)}, u32[]{:S(2)}) %collective-permute-start.11) | collective-permute-done | bytes 6291488 | tf_op jit(solution)/shard_map/ppermute | solution.py:664
  375.2 3.4 fusion.59
  386.4 15.6 %all-gather.12.cloned.1.call-done = bf16[1024,2048]{1,0:T(8,128)(2,1)} async-done(((bf16[256,2048]{1,0:T(8,128)(2,1)}), bf16[1024,2048]{1,0:T(8,128)(2,1)}) %all-gather.12.cloned.1.call-update) | async-done | bytes 4194320 | tf_op jit(solution)/shard_map/all_gather | solution.py:676
  402.0 69.1 %shard_map.314 = (bf16[4,2,128,2048]{3,2,1,0:T(8,128)(2,1)}, bf16[512,2176]{1,0:T(8,128)(2,1)}) custom-call(s32[8]{0:T(128)} %fusion.52.sources, bf16[512,2048]{1,0:T(8,128)(2,1)} %all-gather.14.cloned.1.call-done.rows_in, bf16[4,2,128,2048]{3,2,1,0:T(8,128)(2,1)} %bitcast.131, f32[512,16]{1,0:T(8,128)} %divide_select_fusion.weight, ...), custom_call_target="tpu_custom_call" | custom-call | flops 51539607552 | bytes 50331648 | tf_op jit(solution)/shard_map/pallas_call | solution.py:555
  471.1 69.5 %shard_map.315 = (bf16[4,2,128,2048]{3,2,1,0:T(8,128)(2,1)}, bf16[512,2176]{1,0:T(8,128)(2,1)}) custom-call(s32[8]{0:T(128)} %fusion.52.sources, bf16[512,2048]{1,0:T(8,128)(2,1)} %all-gather.10.cloned.1.call-done.rows_in, bf16[4,2,128,2048]{3,2,1,0:T(8,128)(2,1)} %bitcast.132, ...), custom_call_target="tpu_custom_call", output_to_operand_aliasing={{0}: (12, {})} | custom-call | flops 51539607552 | bytes 50331648 | tf_op jit(solution)/shard_map/pallas_call | solution.py:555
  548.2 37.1 %reduce-scatter.10.cloned.1.call-done = bf16[128,2176]{1,0:T(8,128)(2,1)} async-done(((bf16[512,2176]{1,0:T(8,128)(2,1)}), bf16[128,2176]{1,0:T(8,128)(2,1)}) %reduce-scatter.10.cloned.1.call-update) | async-done | bytes 557072 | tf_op jit(solution)/shard_map/reduce_scatter | solution.py:734
  585.3 47.9 %reduce-scatter.8.cloned.1.call-done = bf16[128,2176]{1,0:T(8,128)(2,1)} async-done(((bf16[512,2176]{1,0:T(8,128)(2,1)}), bf16[128,2176]{1,0:T(8,128)(2,1)}) %reduce-scatter.8.cloned.1.call-update) | async-done | bytes 557072 | tf_op jit(solution)/shard_map/reduce_scatter | solution.py:734
  637.2 3.3 fusion.56
  640.7 80.1 %all-gather.16.cloned.1.call-done = bf16[1024,2048]{1,0:T(8,128)(2,1)} async-done(((bf16[256,2048]{1,0:T(8,128)(2,1)}), bf16[1024,2048]{1,0:T(8,128)(2,1)}) %all-gather.16.cloned.1.call-update) | async-done | bytes 4194320 | tf_op jit(solution)/shard_map/all_gather | solution.py:747
  720.8 5.3 fusion.61
  729.6 16.5 %shard_map.316 = (f32[1024,512]{1,0:T(8,128)}, f32[1024,512]{1,0:T(8,128)}, bf16[1024,512]{1,0:T(8,128)(2,1)S(1)}, f32[2,1024]{1,0:T(2,128)S(1)}) custom-call(bf16[1024,512]{1,0:T(8,128)(2,1)S(1)} %copy-done.11, bf16[1024,512]{1,0:T(8,128)(2,1)} %copy-done.12, bf16[1024,512]{1,0:T(8,128)(2,1)} %copy-done.7, bf16[1024,512]{1,0:T(8,128)(2,1)} %add_convert_fusion.1.grads, ...), custom_call_target="tpu_custom_call" | custom-call | flops 2684354560 | bytes 14680064 | tf_op jit(solution)/shard_map/pallas_call | solution.py:338
  754.2 17.6 %shard_map.317 = (bf16[1024,2048]{1,0:T(8,128)(2,1)}, bf16[1024,1536]{1,0:T(8,128)(2,1)}, f32[1024,48]{1,0:T(8,128)S(1)}) custom-call(f32[1024,512]{1,0:T(8,128)S(1)} %copy-done.15, f32[1024,512]{1,0:T(8,128)} %get-tuple-element.54.key_back, bf16[1024,512]{1,0:T(8,128)(2,1)S(1)} %get-tuple-element.55.value_grads, f32[1024,512]{1,0:T(8,128)} %get-tuple-element.36.query_raw, ...), custom_call_target="tpu_custom_call" | custom-call | flops 6442450944 | bytes 25165824 | tf_op jit(solution)/shard_map/pallas_call | solution.py:418
  775.9 3.2 convolution_convert_fusion
  779.2 22.0 %collective-permute-done.21 = f32[1024,64]{1,0:T(8,128)S(1)} collective-permute-done((f32[1024,64]{1,0:T(8,128)S(1)}, f32[1024,64]{1,0:T(8,128)S(1)}, u32[]{:S(2)}, u32[]{:S(2)}) %collective-permute-start.21) | collective-permute-done | bytes 262176 | tf_op jit(solution)/shard_map/ppermute | solution.py:71
  801.2 67.8 %collective-permute-done.20 = f32[1024,64]{1,0:T(8,128)S(1)} collective-permute-done((f32[1024,64]{1,0:T(8,128)S(1)}, f32[1024,64]{1,0:T(8,128)S(1)}, u32[]{:S(2)}, u32[]{:S(2)}) %collective-permute-start.20) | collective-permute-done | bytes 262176 | tf_op jit(solution)/shard_map/ppermute | solution.py:71
  872.5 3.7 collective-permute-start.22
  881.2 3.7 collective-permute-done.23
  887.0 5.7 collective-permute-done.25
  895.8 9.9 %collective-permute-done.26 = bf16[2,336,512]{2,0,1:T(2,128)(2,1)S(1)} collective-permute-done((bf16[2,336,512]{2,0,1:T(2,128)(2,1)S(1)}, bf16[2,336,512]{2,0,1:T(2,128)(2,1)S(1)}, u32[]{:S(2)}, u32[]{:S(2)}) %collective-permute-start.26) | collective-permute-done | bytes 688160 | tf_op jit(solution)/shard_map/ppermute | solution.py:664
  912.6 4.5 fusion.4
  941.5 30.9 %reduce-scatter.12.cloned.1.call-done = bf16[256,2048]{1,0:T(8,128)(2,1)} async-done(((bf16[1024,2048]{1,0:T(8,128)(2,1)}), bf16[256,2048]{1,0:T(8,128)(2,1)}) %reduce-scatter.12.cloned.1.call-update) | async-done | bytes 1048592 | tf_op jit(solution)/shard_map/reduce_scatter | solution.py:748
  972.3 5.3 fusion.11
  (272 shorter events, 139.2 us)
Async XLA Ops:
  7.2 87.0 %all-gather.8.cloned.1.call-start = ((), (), s32[]{:S(2)}) async-start(), calls=%async_computation.5 | async-start | bytes 7077888 | tf_op jit(solution)/shard_map/all_gather | solution.py:646
  9.5 106.8 %all-gather.18.cloned.1.call-start = ((), (), s32[]{:S(2)}) async-start(), calls=%async_computation.15 | async-start | bytes 2433024 | tf_op jit(solution)/shard_map/all_gather | solution.py:652
  10.2 27.3 %collective-permute-start = (bf16[256,2048]{1,0:T(8,128)(2,1)S(1)}, bf16[256,2048]{1,0:T(8,128)(2,1)S(1)}, u32[]{:S(2)}, u32[]{:S(2)}) collective-permute-start(bf16[256,2048]{1,0:T(8,128)(2,1)S(1)} %fusion.6.refs_0_), channel_id=1, source_target_pairs={{0,1},{1,2},{2,3},{4,5},{5,6},{6,7},{8,9},{9,10},{10,11},{12,13},{... | collective-permute-start | bytes 3145736 | tf_op jit(solution)/shard_map/ppermute | solution.py:41
  15.2 26.6 %collective-permute-start.3 = (bf16[256,2048]{1,0:T(8,128)(2,1)S(1)}, bf16[256,2048]{1,0:T(8,128)(2,1)}, u32[]{:S(2)}, u32[]{:S(2)}) collective-permute-start(bf16[256,2048]{1,0:T(8,128)(2,1)S(1)} %fusion.6.refs_0_), channel_id=1, source_target_pairs={{1,0},{2,1},{3,2},{5,4},{6,5},{7,6},{9,8},{10,9},{11,10},{13,12},{... | collective-permute-start | bytes 3145736 | tf_op jit(solution)/shard_map/ppermute | solution.py:44
  17.3 206.7 %reduce-scatter.6.cloned.1.call-start = ((), (), s32[]{:S(2)}) async-start(), calls=%async_computation.6 | async-start | bytes 5242880 | tf_op jit(solution)/shard_map/reduce_scatter | solution.py:704
  41.8 27.0 %collective-permute-start.4 = (bf16[256,2048]{1,0:T(8,128)(2,1)}, bf16[256,2048]{1,0:T(8,128)(2,1)}, u32[]{:S(2)}, u32[]{:S(2)}) collective-permute-start(bf16[256,2048]{1,0:T(8,128)(2,1)} %collective-permute-done.3.refs_4_), channel_id=1, source_target_pairs={{1,0},{2,1},{5,4},{6,5},{9,8},{10,9},{13,12},{14,13},{17,16},{18,1... | collective-permute-start | bytes 3145736 | tf_op jit(solution)/shard_map/ppermute | solution.py:44
  45.3 29.6 %collective-permute-start.2 = (bf16[256,2048]{1,0:T(8,128)(2,1)}, bf16[256,2048]{1,0:T(8,128)(2,1)}, u32[]{:S(2)}, u32[]{:S(2)}) collective-permute-start(bf16[256,2048]{1,0:T(8,128)(2,1)} %collective-permute-done.1.refs_2_), channel_id=1, source_target_pairs={{2,3},{6,7},{10,11},{14,15},{18,19},{22,23},{26,27},{30,31}} | collective-permute-start | bytes 3145736 | tf_op jit(solution)/shard_map/ppermute | solution.py:41
  68.8 25.4 %collective-permute-start.5 = (bf16[256,2048]{1,0:T(8,128)(2,1)}, bf16[256,2048]{1,0:T(8,128)(2,1)}, u32[]{:S(2)}, u32[]{:S(2)}) collective-permute-start(bf16[256,2048]{1,0:T(8,128)(2,1)} %collective-permute-done.4.refs_5_), channel_id=1, source_target_pairs={{1,0},{5,4},{9,8},{13,12},{17,16},{21,20},{25,24},{29,28}} | collective-permute-start | bytes 3145736 | tf_op jit(solution)/shard_map/ppermute | solution.py:44
  114.0 9.5 collective-permute-start.8
  114.1 9.5 collective-permute-start.7
  115.1 8.5 collective-permute-start.6
  146.4 224.3 %all-gather.10.cloned.1.call-start = ((), (), s32[]{:S(2)}) async-start(), calls=%async_computation.7 | async-start | bytes 2621440 | tf_op jit(solution)/shard_map/all_gather | solution.py:718
  154.1 75.7 %collective-permute-start.9 = (bf16[48,256,256]{2,1,0:T(8,128)(2,1)}, bf16[48,256,256]{2,1,0:T(8,128)(2,1)}, u32[]{:S(2)}, u32[]{:S(2)}) collective-permute-start(bf16[48,256,256]{2,1,0:T(8,128)(2,1)} %constant_dynamic-update-slice_fusion.refs_0_), channel_id=1, source_target_pairs={{0,8},{4,20},{8,0},{12,28},{16,24},{20,4},{24,16},{28,12},{1,9},{5... | collective-permute-start | bytes 18874376 | tf_op jit(solution)/shard_map/ppermute | solution.py:664
  228.2 147.0 %all-gather.14.cloned.1.call-start = ((), (), s32[]{:S(2)}) async-start(), calls=%async_computation.9 | async-start | bytes 2621440 | tf_op jit(solution)/shard_map/all_gather | solution.py:718
  228.3 71.4 %collective-permute-start.10 = (bf16[48,256,256]{2,1,0:T(8,128)(2,1)}, bf16[48,256,256]{2,1,0:T(8,128)(2,1)}, u32[]{:S(2)}, u32[]{:S(2)}) collective-permute-start(bf16[48,256,256]{2,1,0:T(8,128)(2,1)} %constant_dynamic-update-slice_fusion.refs_0_), channel_id=1, source_target_pairs={{0,16},{4,12},{8,24},{12,4},{16,0},{20,28},{24,8},{28,20},{1,17},{... | collective-permute-start | bytes 18874376 | tf_op jit(solution)/shard_map/ppermute | solution.py:664
  229.8 137.2 %collective-permute-start.11 = (bf16[48,256,256]{2,1,0:T(8,128)(2,1)}, bf16[48,256,256]{2,1,0:T(8,128)(2,1)}, u32[]{:S(2)}, u32[]{:S(2)}) collective-permute-start(bf16[48,256,256]{2,1,0:T(8,128)(2,1)} %collective-permute-done.9.refs_1_), channel_id=1, source_target_pairs={{0,16},{4,12},{8,24},{12,4},{16,0},{20,28},{24,8},{28,20},{1,17},{... | collective-permute-start | bytes 18874376 | tf_op jit(solution)/shard_map/ppermute | solution.py:664
  230.4 171.6 %all-gather.12.cloned.1.call-start = ((), (), s32[]{:S(2)}) async-start(), calls=%async_computation.8 | async-start | bytes 5242880 | tf_op jit(solution)/shard_map/all_gather | solution.py:676
  230.4 171.6 %collective-permute-start.12 = (bf16[48,256,256]{2,1,0:T(8,128)(2,1)}, bf16[48,256,256]{2,1,0:T(8,128)(2,1)}, u32[]{:S(2)}, u32[]{:S(2)}) collective-permute-start(bf16[48,256,256]{2,1,0:T(8,128)(2,1)} %constant_dynamic-update-slice_fusion.refs_0_), channel_id=1, source_target_pairs={{0,4},{4,0},{8,12},{12,8},{16,20},{20,16},{24,28},{28,24},{1,5},{5... | collective-permute-start | bytes 18874376 | tf_op jit(solution)/shard_map/ppermute | solution.py:664
  231.0 354.3 %reduce-scatter.10.cloned.1.call-start = ((), (), s32[]{:S(2)}) async-start(), calls=%async_computation.11 | async-start | bytes 2785280 | tf_op jit(solution)/shard_map/reduce_scatter | solution.py:734
  231.3 170.7 %collective-permute-start.13 = (bf16[48,256,256]{2,1,0:T(8,128)(2,1)}, bf16[48,256,256]{2,1,0:T(8,128)(2,1)}, u32[]{:S(2)}, u32[]{:S(2)}) collective-permute-start(bf16[48,256,256]{2,1,0:T(8,128)(2,1)} %collective-permute-done.9.refs_1_), channel_id=1, source_target_pairs={{0,4},{4,0},{8,12},{12,8},{16,20},{20,16},{24,28},{28,24},{1,5},{5... | collective-permute-start | bytes 18874376 | tf_op jit(solution)/shard_map/ppermute | solution.py:664
  299.6 102.4 %collective-permute-start.14 = (bf16[48,256,256]{2,1,0:T(8,128)(2,1)}, bf16[48,256,256]{2,1,0:T(8,128)(2,1)}, u32[]{:S(2)}, u32[]{:S(2)}) collective-permute-start(bf16[48,256,256]{2,1,0:T(8,128)(2,1)} %collective-permute-done.10.refs_2_), channel_id=1, source_target_pairs={{0,4},{4,0},{8,12},{12,8},{16,20},{20,16},{24,28},{28,24},{1,5},{5... | collective-permute-start | bytes 18874376 | tf_op jit(solution)/shard_map/ppermute | solution.py:664
  367.1 35.0 %collective-permute-start.15 = (bf16[48,256,256]{2,1,0:T(8,128)(2,1)}, bf16[48,256,256]{2,1,0:T(8,128)(2,1)}, u32[]{:S(2)}, u32[]{:S(2)}) collective-permute-start(bf16[48,256,256]{2,1,0:T(8,128)(2,1)} %collective-permute-done.11.refs_3_), channel_id=1, source_target_pairs={{0,4},{4,0},{8,12},{12,8},{16,20},{20,16},{24,28},{28,24},{1,5},{5... | collective-permute-start | bytes 18874376 | tf_op jit(solution)/shard_map/ppermute | solution.py:664
  540.6 92.5 %reduce-scatter.8.cloned.1.call-start = ((), (), s32[]{:S(2)}) async-start(), calls=%async_computation.10 | async-start | bytes 2785280 | tf_op jit(solution)/shard_map/reduce_scatter | solution.py:734
  541.4 179.4 %all-gather.16.cloned.1.call-start = ((), (), s32[]{:S(2)}) async-start(), calls=%async_computation.12 | async-start | bytes 5242880 | tf_op jit(solution)/shard_map/all_gather | solution.py:747
  640.5 299.2 %reduce-scatter.14.cloned.1.call-start = ((), (), s32[]{:S(2)}) async-start(), calls=%async_computation.14 | async-start | bytes 5242880 | tf_op jit(solution)/shard_map/reduce_scatter | solution.py:762
  771.9 200.5 %reduce-scatter.12.cloned.1.call-start = ((), (), s32[]{:S(2)}) async-start(), calls=%async_computation.13 | async-start | bytes 5242880 | tf_op jit(solution)/shard_map/reduce_scatter | solution.py:748
  773.2 28.1 %collective-permute-start.21 = (f32[1024,64]{1,0:T(8,128)S(1)}, f32[1024,64]{1,0:T(8,128)S(1)}, u32[]{:S(2)}, u32[]{:S(2)}) collective-permute-start(f32[1024,64]{1,0:T(8,128)S(1)} %pad_maximum_fusion.11), channel_id=1, source_target_pairs={{0,3},{1,0},{2,1},{3,2},{4,7},{5,4},{6,5},{7,6},{8,11},{9,8},{10,9... | collective-permute-start | bytes 786440 | tf_op jit(solution)/shard_map/ppermute | solution.py:71
  774.8 94.2 %collective-permute-start.20 = (f32[1024,64]{1,0:T(8,128)S(1)}, f32[1024,64]{1,0:T(8,128)S(1)}, u32[]{:S(2)}, u32[]{:S(2)}) collective-permute-start(f32[1024,64]{1,0:T(8,128)S(1)} %pad_maximum_fusion.11), channel_id=1, source_target_pairs={{0,2},{1,3},{2,0},{3,1},{4,6},{5,7},{6,4},{7,5},{8,10},{9,11},{10,... | collective-permute-start | bytes 786440 | tf_op jit(solution)/shard_map/ppermute | solution.py:71
  774.8 94.2 %collective-permute-start.19 = (f32[1024,64]{1,0:T(8,128)S(1)}, f32[1024,64]{1,0:T(8,128)S(1)}, u32[]{:S(2)}, u32[]{:S(2)}) collective-permute-start(f32[1024,64]{1,0:T(8,128)S(1)} %pad_maximum_fusion.11), channel_id=1, source_target_pairs={{0,1},{1,2},{2,3},{3,0},{4,5},{5,6},{6,7},{7,4},{8,9},{9,10},{10,1... | collective-permute-start | bytes 786440 | tf_op jit(solution)/shard_map/ppermute | solution.py:71
  872.5 8.7 collective-permute-start.22
  876.2 8.8 collective-permute-start.23
  894.8 11.0 %collective-permute-start.26 = (bf16[2,336,512]{2,0,1:T(2,128)(2,1)S(1)}, bf16[2,336,512]{2,0,1:T(2,128)(2,1)S(1)}, u32[]{:S(2)}, u32[]{:S(2)}) collective-permute-start(bf16[2,336,512]{2,0,1:T(2,128)(2,1)S(1)} %pad_maximum_fusion.8), channel_id=1, source_target_pairs={{0,8},{4,20},{8,0},{12,28},{16,24},{20,4},{24,16},{28,12},{1,9},{5... | collective-permute-start | bytes 2064392 | tf_op jit(solution)/shard_map/ppermute | solution.py:664
  (58 other events, 676.5 us)
Sparse Core Ops, SparseCore 0:
  10.5 48.2 all-gather.7
  61.2 28.1 all-gather.17
  146.5 77.3 reduce-scatter.5
  228.4 46.4 all-gather.9
  276.3 44.6 all-gather.13
  322.5 79.4 all-gather.11
  540.7 44.5 reduce-scatter.9
  587.7 45.3 reduce-scatter.7
  640.6 80.1 all-gather.15
  772.0 112.3 reduce-scatter.13
  886.7 85.5 reduce-scatter.11
